TPU v7x, 32 devices: a whole 2x2x4 slice. The times are simulated.
32 devices in a mesh: sample: 4 (over x, core), freq: 8 (over z, y).
Axes of the slice: x: 2, y: 2, z: 4, core: 2. Of those that a mesh axis runs over, the one named last changes fastest.
Arguments:
- images: bfloat16 [256, 32, 32, 128], P(('sample', 'freq')), may hold values from -6 to 6
- cotangent: bfloat16 [256, 32, 32, 128], P(('sample', 'freq')), may hold values from -6 to 6
- kernel: float32 [3, 3, 128, 128], replicated, may hold values from -0.022097087 to 0.022097087
Outputs:
- outputs: bfloat16 [256, 32, 32, 128], P(('sample', 'freq'))
- kernel_grad: float32 [3, 3, 128, 128], replicated
All inputs are finite; a program needn't handle non-finite values.
Results may differ from a plain program's by a relative error of at most 0.0064.
Values may be sent and summed in bfloat16 or wider, within the bound.
No kernel may reach another device: no remote copies, remote signals or barrier semaphores. Data moves between devices by JAX's collectives and lax.ppermute only.
A program may use at most 128 MiB of HBM per device.

v0:
```python
import math

import jax
import jax.numpy as jnp
from jax import lax
from jax.sharding import PartitionSpec as P

NS_STEPS = 2


HIGHEST = lax.Precision.HIGHEST


def angle_tables(side_cells, half_cells):
    position = jnp.arange(side_cells, dtype=jnp.int32)
    columns = jnp.arange(half_cells, dtype=jnp.int32)
    across = position[:, None] * columns[None, :] % side_cells
    square = position[:, None] * position[None, :] % side_cells
    radians = 2.0 * math.pi / side_cells
    return (radians * across.astype(jnp.float32), radians * square.astype(jnp.float32))


def forward_spectrum(pictures, across_angle, square_angle):
    number = pictures.shape[0]
    side_cells = pictures.shape[1]
    channels = pictures.shape[3]
    half_cells = across_angle.shape[1]
    row_table = jnp.concatenate([jnp.cos(across_angle), -jnp.sin(across_angle)], axis=1)
    partial_sum = jnp.einsum(
        "nhwc,wk->nhkc", pictures, row_table, precision=HIGHEST, preferred_element_type=jnp.float32
    )
    partial_sum = partial_sum.reshape(number, side_cells, 2, half_cells, channels)
    cosine = jnp.cos(square_angle)
    sine_table = jnp.sin(square_angle)
    rotation = jnp.stack([jnp.stack([cosine, sine_table]), jnp.stack([-sine_table, cosine])])
    spectrum = jnp.einsum("abuh,nhbvc->nuvac", rotation, partial_sum, precision=HIGHEST)
    return spectrum.reshape(number, side_cells, half_cells, 2 * channels).astype(jnp.bfloat16)


def inverse_spectrum(spectrum, across_angle, square_angle):
    number = spectrum.shape[0]
    side_cells = spectrum.shape[1]
    half_cells = spectrum.shape[2]
    channels = spectrum.shape[3] // 2
    pieces = spectrum.reshape(number, side_cells, half_cells, 2, channels)
    cosine = jnp.cos(square_angle)
    sine_table = jnp.sin(square_angle)
    rotation = jnp.stack([jnp.stack([cosine, -sine_table]), jnp.stack([sine_table, cosine])])
    column_sum = jnp.einsum(
        "abuh,nuvbc->nhavc", rotation, pieces, precision=HIGHEST, preferred_element_type=jnp.float32
    )
    frequency = jnp.arange(half_cells, dtype=jnp.int32)
    boundary = (frequency == 0) | (frequency == side_cells // 2)
    weights = jnp.where(boundary, 1.0, 2.0).astype(jnp.float32) / (side_cells * side_cells)
    back_table = jnp.concatenate(
        [jnp.cos(across_angle).T * weights[:, None], -jnp.sin(across_angle).T * weights[:, None]],
        axis=0,
    )
    result = jnp.einsum(
        "nhkc,kw->nhwc",
        column_sum.reshape(number, side_cells, 2 * half_cells, channels),
        back_table,
        precision=HIGHEST,
    )
    return result.astype(jnp.bfloat16)


def tap_angles(row_numbers, side_cells, half_cells, tap_count):
    offsets = jnp.arange(tap_count, dtype=jnp.int32) - (tap_count - 1) // 2
    columns = jnp.arange(half_cells, dtype=jnp.int32)
    phases = (
        row_numbers[:, None, None, None] * offsets[None, None, :, None]
        + columns[None, :, None, None] * offsets[None, None, None, :]
    ) % side_cells
    phases = phases.reshape(row_numbers.shape[0] * half_cells, tap_count * tap_count)
    return 2.0 * math.pi / side_cells * phases.astype(jnp.float32)


def skew_matrix(kernel, angles):
    flattened = kernel.reshape(kernel.shape[0] * kernel.shape[1], kernel.shape[2], kernel.shape[3])
    real_part = jnp.einsum("ft,toi->foi", jnp.cos(angles), flattened, precision=HIGHEST)
    imag_part = -jnp.einsum("ft,toi->foi", jnp.sin(angles), flattened, precision=HIGHEST)
    return (real_part - jnp.swapaxes(real_part, 1, 2), imag_part + jnp.swapaxes(imag_part, 1, 2))


def low_multiply(former, latter):
    return jnp.einsum(
        "fij,fjk->fik",
        former.astype(jnp.bfloat16),
        latter.astype(jnp.bfloat16),
        preferred_element_type=jnp.float32,
    )


def full_multiply(former, latter):
    return jnp.einsum("fij,fjk->fik", former, latter, precision=HIGHEST)


def complex_product(former, latter, multiply):
    real_out = multiply(former[0], latter[0]) - multiply(former[1], latter[1])
    imag_out = multiply(former[0], latter[1]) + multiply(former[1], latter[0])
    return (real_out, imag_out)


def adjoint(matrix):
    return (jnp.swapaxes(matrix[0], 1, 2), -jnp.swapaxes(matrix[1], 1, 2))


def cayley_deviation(skew_part):
    deviation = (-skew_part[0], -skew_part[1])
    for iteration in range(NS_STEPS):
        cross_term = complex_product(skew_part, deviation, low_multiply)
        residue = (
            -(skew_part[0] + deviation[0] + cross_term[0]),
            -(skew_part[1] + deviation[1] + cross_term[1]),
        )
        update = complex_product(deviation, residue, low_multiply)
        deviation = (deviation[0] + residue[0] + update[0], deviation[1] + residue[1] + update[1])
    return deviation


def embedded(deviation):
    doubled_real = (2.0 * deviation[0]).astype(jnp.bfloat16)
    doubled_imag = (2.0 * deviation[1]).astype(jnp.bfloat16)
    upper_half = jnp.concatenate([doubled_real, -doubled_imag], axis=2)
    lower_half = jnp.concatenate([doubled_imag, doubled_real], axis=2)
    return jnp.concatenate([upper_half, lower_half], axis=1)


def grad_factor(side_cells, half_cells, total_images):
    frequency = jnp.arange(half_cells, dtype=jnp.int32)
    boundary = (frequency == 0) | (frequency == side_cells // 2)
    return jnp.where(boundary, 2.0, 4.0).astype(jnp.float32) / (
        side_cells * side_cells * total_images
    )


def skew_gradient(spec_grad, deviation):
    conjugate = adjoint(deviation)
    partial_term = complex_product(spec_grad, conjugate, full_multiply)
    partial_term = (spec_grad[0] + partial_term[0], spec_grad[1] + partial_term[1])
    outer_term = complex_product(conjugate, partial_term, full_multiply)
    return (-(partial_term[0] + outer_term[0]), -(partial_term[1] + outer_term[1]))


def kernel_piece(skew_grad, angles, tap_count):
    sym_real = skew_grad[0] - jnp.swapaxes(skew_grad[0], 1, 2)
    sym_imag = skew_grad[1] + jnp.swapaxes(skew_grad[1], 1, 2)
    piece_sum = jnp.einsum(
        "ft,foi->toi", jnp.cos(angles), sym_real, precision=HIGHEST
    ) - jnp.einsum("ft,foi->toi", jnp.sin(angles), sym_imag, precision=HIGHEST)
    return piece_sum.reshape(tap_count, tap_count, sym_real.shape[1], sym_real.shape[2])


def per_device(images, cotangent, kernel):
    side_cells = images.shape[1]
    channels = images.shape[3]
    half_cells = side_cells // 2 + 1
    tap_count = kernel.shape[0]
    across_angle, square_angle = angle_tables(side_cells, half_cells)
    image_spectrum = forward_spectrum(images, across_angle, square_angle)
    tangent_spectrum = forward_spectrum(cotangent, across_angle, square_angle)
    image_owned, tangent_owned = (
        lax.all_to_all(image_spectrum, "freq", split_axis=1, concat_axis=0, tiled=True),
        lax.all_to_all(tangent_spectrum, "freq", split_axis=1, concat_axis=0, tiled=True),
    )
    group_count = image_owned.shape[0]
    row_count = image_owned.shape[1]
    owned_count = row_count * half_cells
    row_numbers = lax.axis_index("freq") * row_count + jnp.arange(row_count, dtype=jnp.int32)
    angles = tap_angles(row_numbers, side_cells, half_cells, tap_count)
    skew_part = skew_matrix(kernel, angles)
    deviation = cayley_deviation(skew_part)
    operator = embedded(deviation)
    image_rows = image_owned.reshape(group_count, owned_count, 2 * channels)
    tangent_rows = tangent_owned.reshape(group_count, owned_count, 2 * channels)
    answer = jnp.einsum("nfj,fkj->nfk", image_rows, operator, preferred_element_type=jnp.float32)
    answer = (answer + image_rows.astype(jnp.float32)).astype(jnp.bfloat16)
    answer = answer.reshape(group_count, row_count, half_cells, 2 * channels)
    returned = lax.all_to_all(answer, "freq", split_axis=0, concat_axis=1, tiled=True)
    outputs = inverse_spectrum(returned, across_angle, square_angle)
    outer_sum = jnp.einsum(
        "nfk,nfj->fkj", tangent_rows, image_rows, preferred_element_type=jnp.float32
    )
    total_images = group_count * lax.axis_size("sample")
    factor = jnp.tile(grad_factor(side_cells, half_cells, total_images), row_count)
    grad_real = (outer_sum[:, :channels, :channels] + outer_sum[:, channels:, channels:]) * factor[
        :, None, None
    ]
    grad_imag = (outer_sum[:, channels:, :channels] - outer_sum[:, :channels, channels:]) * factor[
        :, None, None
    ]
    spec_grad = lax.psum((grad_real, grad_imag), "sample")
    piece_sum = kernel_piece(skew_gradient(spec_grad, deviation), angles, tap_count)
    kernel_grad = lax.psum(piece_sum, "freq")
    return (outputs, kernel_grad)


def solution(mesh):
    placed = (P(("sample", "freq"), None, None, None), P(("sample", "freq"), None, None, None), P())
    return jax.shard_map(
        per_device,
        mesh=mesh,
        in_specs=placed,
        out_specs=(P(("sample", "freq"), None, None, None), P()),
        check_vma=False,
    )
```

profile of v0, /device:TPU:0, one launch (start us, length us, event | category | flops | bytes accessed | tf_op | source)
XLA Modules:
  0.0 616.4 jit_solution(4949149420963267916)
XLA Ops:
  25.9 7.5 %all-to-all-start.2 = ((bf16[8,32,17,256]{3,0,2,1:T(8,128)(2,1)}), bf16[8,32,17,256]{3,0,2,1:T(8,128)(2,1)}, u32[]{:S(2)}, u32[]{:S(2)}) async-start(bf16[8,32,17,256]{3,0,2,1:T(8,128)(2,1)} %reshape.255), calls=%async_computation.2 | async-start | bytes 4456448 | tf_op jit(solution)/shard_map/all_to_all | solution.py:165
  61.4 8.9 %fusion.120 = (f32[68,128,128]{2,1,0:T(8,128)}, f32[68,128,128]{2,1,0:T(8,128)}) fusion(f32[68,128,128]{1,2,0:T(8,128)} %copy.454, f32[68,128,128]{2,0,1:T(8,128)} %copy-done.16), kind=kLoop, calls=%fused_computation.177 | loop fusion | flops 3342336 | bytes 17825792 | tf_op jit(solution)/shard_map/neg | solution.py:110
  82.5 10.9 %negate_convert_fusion = (bf16[68,128,128]{2,1,0:T(8,128)(2,1)}, f32[68,128,128]{2,1,0:T(8,128)S(1)}, bf16[68,128,128]{2,1,0:T(8,128)(2,1)}, bf16[68,128,128]{2,1,0:T(8,128)(2,1)}) fusion(f32[68,128,128]{1,2,0:T(8,128)} %copy.449, f32[68,128,128]{2,0,1:T(8,128)} %fusion.51, f32[68,128,128]{2,1,0:T(8,128)} %get-tuple-element.9), kind=kLoop, calls=%fused_computation.9 | loop fusion | flops 6684672 | bytes 24510464 | tf_op jit(solution)/shard_map/convert_element_type | solution.py:90
  141.1 13.2 %fusion.119 = (bf16[68,128,128]{2,1,0:T(8,128)(2,1)S(1)}, f32[68,128,128]{2,1,0:T(8,128)}, f32[68,128,128]{2,1,0:T(8,128)}) fusion(f32[68,128,128]{2,1,0:T(8,128)} %copy.465, f32[68,128,128]{2,1,0:T(8,128)} %get-tuple-element.27, f32[68,128,128]{2,1,0:T(8,128)} %get-tuple-element.9, f32[68,128,128]{2,1,0:T(8,128)} %fusion.125, ...), kind=kOutput, calls=%fused_computation.176 | convolution fusion | flops 294125568 | bytes 35651584 | tf_op jit(solution)/shard_map/fij,fjk->fik/dot_general | solution.py:87
  163.1 7.2 %fusion.121 = (bf16[68,128,128]{2,1,0:T(8,128)(2,1)S(1)}, f32[68,128,128]{2,1,0:T(8,128)}) fusion(f32[68,128,128]{2,1,0:T(8,128)} %fusion.57, bf16[68,128,128]{2,1,0:T(8,128)(2,1)S(1)} %copy-done.4, bf16[68,128,128]{2,1,0:T(8,128)(2,1)S(1)} %copy-done.22, f32[68,128,128]{2,1,0:T(8,128)} %fusion.15, f32[68,128,128]{2,1,0:T(8,128)S(1)} %bitcast.199), kind=kOutput, calls=%fused_computation.178 | convolution fusion | flops 290783232 | bytes 24510464 | tf_op jit(solution)/shard_map/fij,fjk->fik/dot_general | solution.py:87
  171.7 6.4 %fusion.45 = (bf16[68,128,128]{2,1,0:T(8,128)(2,1)}, f32[68,128,128]{2,1,0:T(8,128)}) fusion(f32[68,128,128]{2,1,0:T(8,128)S(1)} %bitcast.189, f32[68,128,128]{2,1,0:T(8,128)S(1)} %bitcast.205, f32[68,128,128]{2,1,0:T(8,128)} %fusion.126, bf16[68,128,128]{2,1,0:T(8,128)(2,1)S(1)} %copy-done.6, bf16[68,128,128]{2,1,0:T(8,128)(2,1)S(1)} %get-tuple-element.28), kind=kOutput, calls=%fused_computation.71 | convolution fusion | flops 290783232 | bytes 24510464 | tf_op jit(solution)/shard_map/fij,fjk->fik/dot_general | solution.py:87
  204.5 7.3 %multiply_convert_fusion.1 = (bf16[68,128,128]{2,1,0:T(8,128)(2,1)}, f32[68,128,128]{2,1,0:T(8,128)}) fusion(f32[68,128,128]{2,1,0:T(8,128)} %fusion.54, bf16[68,128,128]{2,1,0:T(8,128)(2,1)S(1)} %copy-done.9, bf16[68,128,128]{2,1,0:T(8,128)(2,1)S(1)} %copy-done.20, f32[68,128,128]{2,1,0:T(8,128)S(1)} %bitcast.207, f32[68,128,128]{2,1,0:T(8,128)S(1)} %add_negate_fusion.3), kind=kOutput, calls=%fused_computation.51 | convolution fusion | flops 290783232 | bytes 24510464 | tf_op jit(solution)/shard_map/fij,fjk->fik/dot_general | solution.py:87
  211.8 6.9 %fusion.118 = (bf16[68,128,128]{2,1,0:T(8,128)(2,1)}, bf16[68,128,128]{2,1,0:T(8,128)(2,1)}, f32[68,128,128]{2,1,0:T(8,128)}) fusion(f32[68,128,128]{2,1,0:T(8,128)} %get-tuple-element.7, f32[68,128,128]{2,1,0:T(8,128)S(1)} %bitcast.203, f32[68,128,128]{2,1,0:T(8,128)S(1)} %bitcast.191, f32[68,128,128]{2,1,0:T(8,128)} %fusion.127, ...), kind=kOutput, calls=%fused_computation.175 | convolution fusion | flops 296353792 | bytes 33423360 | tf_op jit(solution)/shard_map/fij,fjk->fik/dot_general | solution.py:87
  222.1 12.7 %all-to-all-done = bf16[8,32,17,256]{3,0,2,1:T(8,128)(2,1)} async-done(((bf16[8,32,17,256]{3,0,2,1:T(8,128)(2,1)}), bf16[8,32,17,256]{3,0,2,1:T(8,128)(2,1)}, u32[]{:S(2)}, u32[]{:S(2)}) %all-to-all-start) | async-done | bytes 2228256 | tf_op jit(solution)/shard_map/all_to_all | solution.py:164
  244.2 8.1 %fusion.26 = bf16[64,68,256]{2,0,1:T(8,128)(2,1)S(1)} fusion(bf16[64,68,256]{2,0,1:T(8,128)(2,1)} %bitcast.216, bf16[68,128,128]{2,1,0:T(8,128)(2,1)} %get-tuple-element.33, bf16[68,128,128]{2,1,0:T(8,128)(2,1)} %get-tuple-element.5, bf16[68,128,128]{2,1,0:T(8,128)(2,1)} %get-tuple-element.4), kind=kOutput, calls=%fused_computation.39 | convolution fusion | flops 609419264 | bytes 11141120 | tf_op jit(solution)/shard_map/nfj,fkj->nfk/dot_general | solution.py:177
  260.0 14.9 %fusion.19 = f32[68,128,128]{1,2,0:T(8,128)} fusion(f32[68,128,128]{2,1,0:T(8,128)} %get-tuple-element.35, f32[68,128,128]{2,1,0:T(8,128)} %get-tuple-element.32, f32[68,128,128]{1,2,0:T(8,128)} %copy.459, f32[68,128,128]{2,1,0:T(8,128)} %get-tuple-element.30, f32[68,128,128]{1,2,0:T(8,128)} %copy.460, f32[68,128,128]{1,2,0:T(8,128)} %add.268, ...), kind=kLoop, calls=%fused_computation.27 | loop fusion | flops 11141120 | bytes 35651584 | tf_op jit(solution)/shard_map/neg | solution.py:106
  274.9 35.4 %all-to-all-done.1 = bf16[64,4,17,256]{3,1,2,0:T(4,128)(2,1)} async-done(((bf16[64,4,17,256]{3,1,2,0:T(4,128)(2,1)}), bf16[64,4,17,256]{3,1,2,0:T(4,128)(2,1)}, u32[]{:S(2)}, u32[]{:S(2)}) %all-to-all-start.1) | async-done | bytes 2228256 | tf_op jit(solution)/shard_map/all_to_all | solution.py:180
  319.3 85.8 %all-reduce.6.cloned.1.call-done = (f32[68,128,128]{2,1,0:T(8,128)}, f32[68,128,128]{2,1,0:T(8,128)}) async-done(((f32[68,128,128]{2,1,0:T(8,128)}, f32[68,128,128]{2,1,0:T(8,128)}), (f32[68,128,128]{2,1,0:T(8,128)}, f32[68,128,128]{2,1,0:T(8,128)})) %all-reduce.6.cloned.1.call-update) | async-done | bytes 8912912 | tf_op jit(solution)/shard_map/psum | solution.py:193
  405.1 15.2 %fusion.131 = f32[68,128,128]{2,1,0:T(8,128)} fusion(f32[68,128,128]{2,1,0:T(8,128)} %get-tuple-element.3, f32[68,128,128]{1,2,0:T(8,128)} %fusion.19), kind=kOutput, calls=%fused_computation.188 | convolution fusion | flops 1711276032 | bytes 13369344 | tf_op jit(solution)/shard_map/fij,fjk->fik/dot_general | solution.py:96
  420.3 11.1 %fusion.129 = f32[68,128,128]{2,1,0:T(8,128)} fusion(f32[68,128,128]{2,1,0:T(8,128)S(1)} %copy-done.19, f32[68,128,128]{2,1,0:T(8,128)S(1)} %bitcast.195), kind=kOutput, calls=%fused_computation.186 | convolution fusion | flops 1711276032 | bytes 13369344 | tf_op jit(solution)/shard_map/fij,fjk->fik/dot_general | solution.py:96
  431.4 13.2 %add_add_fusion = f32[68,128,128]{2,1,0:T(8,128)S(1)} fusion(f32[68,128,128]{2,1,0:T(8,128)} %get-tuple-element.2, f32[68,128,128]{2,1,0:T(8,128)} %fusion.131, f32[68,128,128]{2,1,0:T(8,128)S(1)} %bitcast.195), kind=kOutput, calls=%fused_computation.48 | convolution fusion | flops 1713504256 | bytes 17825792 | tf_op jit(solution)/shard_map/fij,fjk->fik/dot_general | solution.py:96
  444.6 8.9 %fusion.132 = f32[68,128,128]{2,1,0:T(8,128)} fusion(f32[68,128,128]{2,1,0:T(8,128)S(1)} %bitcast.195, f32[68,128,128]{2,1,0:T(8,128)S(1)} %add_add_fusion), kind=kOutput, calls=%fused_computation.189 | convolution fusion | flops 1711276032 | bytes 13369344 | tf_op jit(solution)/shard_map/fij,fjk->fik/dot_general | solution.py:96
  453.6 14.3 %subtract_add_fusion = f32[68,128,128]{2,1,0:T(8,128)} fusion(f32[68,128,128]{2,1,0:T(8,128)} %get-tuple-element.3, f32[68,128,128]{2,1,0:T(8,128)} %fusion.129, f32[68,128,128]{2,1,0:T(8,128)} %get-tuple-element.2, f32[68,128,128]{1,2,0:T(8,128)S(1)} %bitcast.193), kind=kOutput, calls=%fused_computation.49 | convolution fusion | flops 1713504256 | bytes 22282240 | tf_op jit(solution)/shard_map/fij,fjk->fik/dot_general | solution.py:96
  467.9 10.6 %fusion.130 = f32[68,128,128]{2,1,0:T(8,128)} fusion(f32[68,128,128]{2,1,0:T(8,128)S(1)} %bitcast.195, f32[68,128,128]{2,1,0:T(8,128)} %subtract_add_fusion), kind=kOutput, calls=%fused_computation.187 | convolution fusion | flops 1711276032 | bytes 13369344 | tf_op jit(solution)/shard_map/fij,fjk->fik/dot_general | solution.py:96
  478.5 11.8 %add_negate_fusion = f32[68,128,128]{2,1,0:T(8,128)} fusion(f32[68,128,128]{2,1,0:T(8,128)S(1)} %add_add_fusion, f32[68,128,128]{2,1,0:T(8,128)} %fusion.132, f32[68,128,128]{1,2,0:T(8,128)S(1)} %bitcast.193, f32[68,128,128]{2,1,0:T(8,128)} %subtract_add_fusion), kind=kOutput, calls=%fused_computation.46 | convolution fusion | flops 1714618368 | bytes 22282240 | tf_op jit(solution)/shard_map/fij,fjk->fik/dot_general | solution.py:96
  490.3 9.4 %add_negate_fusion.1 = f32[68,128,128]{2,1,0:T(8,128)} fusion(f32[68,128,128]{2,1,0:T(8,128)S(1)} %bitcast.201, f32[68,128,128]{2,1,0:T(8,128)S(1)} %copy-done.23, f32[68,128,128]{1,2,0:T(8,128)S(1)} %bitcast.193, f32[68,128,128]{2,1,0:T(8,128)S(1)} %add_add_fusion), kind=kOutput, calls=%fused_computation.47 | convolution fusion | flops 1714618368 | bytes 22282240 | tf_op jit(solution)/shard_map/fij,fjk->fik/dot_general | solution.py:96
  505.6 6.9 %bitcast_subtract_fusion = f32[68,128,128]{2,1,0:T(8,128)} fusion(f32[68,128,128]{2,1,0:T(8,128)} %add_negate_fusion.1, f32[68,128,128]{1,2,0:T(8,128)} %copy.512), kind=kLoop, calls=%fused_computation.25 | loop fusion | flops 1114112 | bytes 13369344 | tf_op jit(solution)/shard_map/sub | solution.py:147
  538.8 7.3 %convert_bitcast_fusion = bf16[8,32,32,128]{3,2,1,0:T(8,128)(2,1)} fusion(f32[8,32,34,128]{3,1,2,0:T(8,128)S(1)} %bitcast.208, f32[17,32]{0,1:T(8,128)S(1)} %get-tuple-element.25, f32[17,32]{0,1:T(8,128)S(1)} %get-tuple-element.24), kind=kOutput, calls=%fused_computation.69 | convolution fusion | flops 428868672 | bytes 6557952 | tf_op jit(solution)/shard_map/nhkc,kw->nhwc/dot_general | solution.py:59
  546.1 61.3 %all-reduce.4.cloned.1.call-done = f32[3,3,128,128]{3,2,1,0:T(8,128)} async-done(((f32[3,3,128,128]{3,2,1,0:T(8,128)}), f32[3,3,128,128]{3,2,1,0:T(8,128)}) %all-reduce.4.cloned.1.call-update) | async-done | bytes 589840 | tf_op jit(solution)/shard_map/psum | solution.py:195
  (196 shorter events, 206.3 us)
Async XLA Ops:
  19.8 14.5 %copy-start.26 = (f32[3,3,128,128]{3,2,1,0:T(8,128)S(1)}, f32[3,3,128,128]{3,2,1,0:T(8,128)}, u32[]{:S(2)}) copy-start(f32[3,3,128,128]{3,2,1,0:T(8,128)} %param.5) | copy-start | bytes 1769476
  25.9 152.3 %all-to-all-start.2 = ((bf16[8,32,17,256]{3,0,2,1:T(8,128)(2,1)}), bf16[8,32,17,256]{3,0,2,1:T(8,128)(2,1)}, u32[]{:S(2)}, u32[]{:S(2)}) async-start(bf16[8,32,17,256]{3,0,2,1:T(8,128)(2,1)} %reshape.255), calls=%async_computation.2 | async-start | bytes 4456448 | tf_op jit(solution)/shard_map/all_to_all | solution.py:165
  135.1 28.0 %slice-start.10 = ((s8[4456448]{0:T(1024)(128)(4,1)}), s8[262144]{0:T(1024)(128)(4,1)S(1)}, s32[]{:S(2)}) async-start(s8[4456448]{0:T(1024)(128)(4,1)} %bitcast.198), calls=%async_computation.15 | async-start | bytes 524288
  141.1 13.2 %copy-start.15 = (bf16[68,128,128]{2,1,0:T(8,128)(2,1)S(1)}, bf16[68,128,128]{2,1,0:T(8,128)(2,1)}, u32[]{:S(2)}) copy-start(bf16[68,128,128]{2,1,0:T(8,128)(2,1)} %convert_element_type.152) | copy-start | bytes 6684676
  141.1 21.9 %slice-start.11 = ((s8[4456448]{0:T(1024)(128)(4,1)}), s8[4194304]{0:T(1024)(128)(4,1)S(1)}, s32[]{:S(2)}) async-start(s8[4456448]{0:T(1024)(128)(4,1)} %bitcast.198), calls=%async_computation.16 | async-start | bytes 8388608
  157.6 14.1 %slice-start = ((s8[4456448]{0:T(1024)(128)(4,1)}), s8[4194304]{0:T(1024)(128)(4,1)S(1)}, s32[]{:S(2)}) async-start(s8[4456448]{0:T(1024)(128)(4,1)} %bitcast.188), calls=%async_computation.5 | async-start | bytes 8388608
  157.6 14.1 %slice-start.16 = ((s8[4456448]{0:T(1024)(128)(4,1)}), s8[262144]{0:T(1024)(128)(4,1)S(1)}, s32[]{:S(2)}) async-start(s8[4456448]{0:T(1024)(128)(4,1)} %bitcast.204), calls=%async_computation.21 | async-start | bytes 524288
  178.1 56.6 %all-to-all-start = ((bf16[8,32,17,256]{3,0,2,1:T(8,128)(2,1)}), bf16[8,32,17,256]{3,0,2,1:T(8,128)(2,1)}, u32[]{:S(2)}, u32[]{:S(2)}) async-start(bf16[8,32,17,256]{3,0,2,1:T(8,128)(2,1)} %reshape.254), calls=%async_computation | async-start | bytes 4456448 | tf_op jit(solution)/shard_map/all_to_all | solution.py:164
  184.2 220.9 %all-reduce.6.cloned.1.call-start = ((), (), s32[]{:S(2)}) async-start(), calls=%async_computation.4 | async-start | bytes 17825792 | tf_op jit(solution)/shard_map/psum | solution.py:193
  189.6 14.9 %slice-start.18 = ((s8[4456448]{0:T(1024)(128)(4,1)}), s8[4194304]{0:T(1024)(128)(4,1)S(1)}, s32[]{:S(2)}) async-start(s8[4456448]{0:T(1024)(128)(4,1)} %bitcast.206), calls=%async_computation.23 | async-start | bytes 8388608
  201.5 10.3 %slice-start.2 = ((s8[4456448]{0:T(1024)(128)(4,1)}), s8[4194304]{0:T(1024)(128)(4,1)S(1)}, s32[]{:S(2)}) async-start(s8[4456448]{0:T(1024)(128)(4,1)} %bitcast.190), calls=%async_computation.7 | async-start | bytes 8388608
  201.5 10.3 %slice-start.14 = ((s8[4456448]{0:T(1024)(128)(4,1)}), s8[4194304]{0:T(1024)(128)(4,1)S(1)}, s32[]{:S(2)}) async-start(s8[4456448]{0:T(1024)(128)(4,1)} %bitcast.202), calls=%async_computation.19 | async-start | bytes 8388608
  255.4 55.0 %all-to-all-start.1 = ((bf16[64,4,17,256]{3,1,2,0:T(4,128)(2,1)}), bf16[64,4,17,256]{3,1,2,0:T(4,128)(2,1)}, u32[]{:S(2)}, u32[]{:S(2)}) async-start(bf16[64,4,17,256]{3,1,2,0:T(4,128)(2,1)} %copy.494), calls=%async_computation.1 | async-start | bytes 4456448 | tf_op jit(solution)/shard_map/all_to_all | solution.py:180
  259.7 347.7 %all-reduce.4.cloned.1.call-start = ((), (), s32[]{:S(2)}) async-start(), calls=%async_computation.3 | async-start | bytes 1179648 | tf_op jit(solution)/shard_map/psum | solution.py:195
  313.9 106.4 %slice-start.6 = ((s8[4456448]{0:T(1024)(128)(4,1)}), s8[262144]{0:T(1024)(128)(4,1)S(1)}, s32[]{:S(2)}) async-start(s8[4456448]{0:T(1024)(128)(4,1)} %bitcast.194), calls=%async_computation.11 | async-start | bytes 524288
  405.1 15.2 %slice-start.7 = ((s8[4456448]{0:T(1024)(128)(4,1)}), s8[4194304]{0:T(1024)(128)(4,1)S(1)}, s32[]{:S(2)}) async-start(s8[4456448]{0:T(1024)(128)(4,1)} %bitcast.194), calls=%async_computation.12 | async-start | bytes 8388608
  405.1 15.2 %copy-start.19 = (f32[68,128,128]{2,1,0:T(8,128)S(1)}, f32[68,128,128]{2,1,0:T(8,128)}, u32[]{:S(2)}) copy-start(f32[68,128,128]{2,1,0:T(8,128)} %get-tuple-element.3) | copy-start | bytes 13369348
  420.3 33.3 %slice-start.4 = ((s8[4456448]{0:T(1024)(128)(4,1)}), s8[4194304]{0:T(1024)(128)(4,1)S(1)}, s32[]{:S(2)}) async-start(s8[4456448]{0:T(1024)(128)(4,1)} %bitcast.192), calls=%async_computation.9 | async-start | bytes 8388608
  431.4 22.2 %slice-start.5 = ((s8[4456448]{0:T(1024)(128)(4,1)}), s8[262144]{0:T(1024)(128)(4,1)S(1)}, s32[]{:S(2)}) async-start(s8[4456448]{0:T(1024)(128)(4,1)} %bitcast.192), calls=%async_computation.10 | async-start | bytes 524288
  467.9 22.4 %slice-start.12 = ((s8[4456448]{0:T(1024)(128)(4,1)}), s8[4194304]{0:T(1024)(128)(4,1)S(1)}, s32[]{:S(2)}) async-start(s8[4456448]{0:T(1024)(128)(4,1)} %bitcast.200), calls=%async_computation.17 | async-start | bytes 8388608
  478.5 11.8 %slice-start.13 = ((s8[4456448]{0:T(1024)(128)(4,1)}), s8[262144]{0:T(1024)(128)(4,1)S(1)}, s32[]{:S(2)}) async-start(s8[4456448]{0:T(1024)(128)(4,1)} %bitcast.200), calls=%async_computation.18 | async-start | bytes 524288
  478.5 11.8 %copy-start.23 = (f32[68,128,128]{2,1,0:T(8,128)S(1)}, f32[68,128,128]{2,1,0:T(8,128)}, u32[]{:S(2)}) copy-start(f32[68,128,128]{2,1,0:T(8,128)} %fusion.130) | copy-start | bytes 13369348
  512.5 15.7 %slice-start.20 = ((s8[4456448]{0:T(1024)(128)(4,1)}), s8[262144]{0:T(1024)(128)(4,1)S(1)}, s32[]{:S(2)}) async-start(s8[4456448]{0:T(1024)(128)(4,1)} %bitcast.209), calls=%async_computation.25 | async-start | bytes 524288
  538.1 71.3 %copy-start.1 = (bf16[8,32,32,128]{3,2,1,0:T(8,128)(2,1)S(1)}, bf16[8,32,32,128]{3,2,1,0:T(8,128)(2,1)}, u32[]{:S(2)}) copy-start(bf16[8,32,32,128]{3,2,1,0:T(8,128)(2,1)} %param.4) | copy-start | bytes 6291460
  (37 other events, 180.2 us)
Sparse Core Ops, SparseCore 0:
  244.3 160.7 all-reduce.5
  534.3 73.0 all-reduce.3
where the time goes:
time: 624 us; the launch traced here: 616 us
  matrix products  231 us (37%)
  waiting for transfers between devices  195 us (31%)
  local copies, waits for them, and re-layouts  94.3 us (15%)
  other arithmetic  62.4 us (10%)
  starting transfers between devices  18.2 us (3%)
  between operations  14.9 us (2%)
    dot_general x8, matrix products, full_multiply(): return jnp.einsum('fij,fjk->fik', former, latter, precision=HIGHEST)  94.6 us
    psum x1, waiting for transfers between devices, per_device(): spec_grad = lax.psum((grad_real, grad_imag), 'sample')  85.8 us
    dot_general x16, matrix products, low_multiply(): jnp.einsum('fij,fjk->fik', former.astype(jnp.bfloat16), latter.astype(jnp...  82.1 us
    psum x1, waiting for transfers between devices, per_device(): kernel_grad = lax.psum(piece_sum, 'freq')  61.3 us
    all_to_all x1, waiting for transfers between devices, per_device(): lax.all_to_all(answer, 'freq', split_axis=0, concat_axis=1, tiled=True)  35.4 us
    convert_element_type x4, local copies, waits for them, and re-layouts, forward_spectrum(): spectrum.reshape(number, side_cells, half_cells, 2 * channels)  18.3 us
    neg x1, other arithmetic, adjoint(): return (jnp.swapaxes(matrix[0], 1, 2), -jnp.swapaxes(matrix[1], 1, 2))  14.9 us
    unnamed x113, local copies, waits for them, and re-layouts  13.2 us
  transfers between devices with their start and end apart: 5, of which 4 were waited for; matrix products, arithmetic and copies ran while one was open for 36% of the time, Pallas kernels for 0%

commit v1 on v0

v1 whole, which is shorter than its diff:
```python
import functools
import math

import jax
import jax.numpy as jnp
import numpy as np
from jax import lax
from jax.experimental import pallas as pl
from jax.experimental.pallas import tpu as pltpu
from jax.sharding import PartitionSpec as P

AXES = ("sample", "freq")
APPLICATIONS = 7
CHAINS = 2
VMEM_LIMIT = 56 * 1024 * 1024


def split_table(table):
    high = table.astype(jnp.bfloat16)
    low = (table - high.astype(np.float64)).astype(jnp.bfloat16)
    return high, low


def forward_table(number, side):
    place = np.arange(side)
    table = np.zeros((side, side))
    table[0] = 1.0
    table[1] = np.cos(np.pi * place)
    for slot in range(1, side // 2):
        angle = 2.0 * math.pi * ((slot * place) % side) / side
        table[2 * slot] = np.cos(angle)
        table[2 * slot + 1] = -np.sin(angle)
    full = np.einsum("kw,nm->knmw", table, np.eye(number))
    return full.reshape(side * number, number * side)


def inverse_table(number, side):
    place = np.arange(side)
    table = np.zeros((side, side))
    table[:, 0] = 2.0 / side
    table[:, 1] = 2.0 / side * np.cos(np.pi * place)
    for slot in range(1, side // 2):
        angle = 2.0 * math.pi * ((slot * place) % side) / side
        table[:, 2 * slot] = 4.0 / side * np.cos(angle)
        table[:, 2 * slot + 1] = -4.0 / side * np.sin(angle)
    full = np.einsum("wk,nm->nwkm", table, np.eye(number))
    return full.reshape(number * side, side * number)


def slot_factors(side):
    rows = [[1.0, -1.0, 0.0, 1.0 / side]]
    for slot in range(1, side // 2):
        angle = 2.0 * math.pi * slot / side
        rows.append([math.cos(angle), math.cos(angle), math.sin(angle), 2.0 / side])
    table = np.array(rows)
    weighted = table[:, :3] * table[:, 3:]
    return np.concatenate([table, weighted], axis=1).astype(np.float32)


def dot(left, right):
    return jnp.dot(left, right, preferred_element_type=jnp.float32)


def main_kernel(
    scale,
    factor_ref,
    x_ref,
    t_ref,
    kernel_ref,
    high_ref,
    low_ref,
    dev_ref,
    grad_ref,
    base_ref,
    held_ref,
    weight_ref,
    taps_ref,
    sums_ref,
):
    number, side, _, channels = x_ref.shape
    slots = side // 2
    wide = 2 * channels

    for a in range(3):
        flipped = [kernel_ref[a, b].T - kernel_ref[2 - a, 2 - b] for b in range(3)]
        taps_ref[a, 0] = -flipped[1]
        taps_ref[a, 1] = -(flipped[2] + flipped[0])
        taps_ref[a, 2] = flipped[2] - flipped[0]
    sums_ref[...] = jnp.zeros_like(sums_ref)

    def transform(h, carry):
        rows = jnp.concatenate(
            [
                x_ref[:, h].reshape(number * side, channels),
                t_ref[:, h].reshape(number * side, channels),
            ],
            axis=1,
        )
        result = dot(high_ref[...], rows) + dot(low_ref[...], rows)
        result = result.reshape(slots, 2, number, wide)
        base_ref[:, h, :number, :channels] = result[:, 0, :, :channels]
        base_ref[:, h, :number, channels:] = result[:, 1, :, :channels]
        base_ref[:, h, number:, :channels] = result[:, 0, :, channels:]
        base_ref[:, h, number:, channels:] = result[:, 1, :, channels:]
        return carry

    lax.fori_loop(0, side, transform, 0, unroll=2)

    def store_held(chain, parity, start, rows):
        held = rows.astype(jnp.bfloat16)
        count = rows.shape[0]
        held_ref[chain, parity, start + 1 : start + 1 + count] = held
        if start == 0:
            held_ref[chain, parity, side + 1] = held[0]
        if start + count == side:
            held_ref[chain, parity, 0] = held[count - 1]

    def prepare(chain, slot):
        cos_top, cos_low, sine = (factor_ref[slot, j] for j in range(3))
        for a in range(3):
            first, second = taps_ref[a, 0], taps_ref[a, 1]
            cross = sine * taps_ref[a, 2]
            row = a * wide
            weight_ref[chain, row : row + channels, :channels] = (
                first + cos_top * second
            ).astype(jnp.bfloat16)
            weight_ref[chain, row + channels : row + wide, channels:] = (
                first + cos_low * second
            ).astype(jnp.bfloat16)
            weight_ref[chain, row : row + channels, channels:] = cross.astype(jnp.bfloat16)
            weight_ref[chain, row + channels : row + wide, :channels] = (-cross).astype(
                jnp.bfloat16
            )
        store_held(chain, 0, 0, base_ref[slot])

    def apply(chain, slot, step):
        parity = step % 2
        left = jnp.concatenate(
            [
                held_ref[chain, parity, 2 - a : 2 - a + side].reshape(side * 2 * number, wide)
                for a in range(3)
            ],
            axis=1,
        )
        moved = dot(left, weight_ref[chain]).reshape(side, 2 * number, wide)
        base = base_ref[slot]
        x_new = base[:, :number] + moved[:, :number]
        if step % 2 == 0:
            t_new = moved[:, number:] - base[:, number:]
        else:
            t_new = moved[:, number:] + base[:, number:]
        return moved, x_new, t_new

    def finish(chain, slot, moved, x_new, t_new):
        dev_ref[:, 2 * slot] = moved[:, :number, :channels]
        dev_ref[:, 2 * slot + 1] = moved[:, :number, channels:]
        left = t_new.reshape(side * number, wide).astype(jnp.bfloat16)
        around = jnp.concatenate([x_new[side - 1 :], x_new, x_new[:1]], axis=0)
        weight, top, low, sine = (factor_ref[slot, j] for j in range(3, 7))
        for a in range(3):
            right = around[2 - a : 2 - a + side].reshape(side * number, wide).astype(jnp.bfloat16)
            outer = lax.dot_general(
                left, right, (((0,), (0,)), ((), ())), preferred_element_type=jnp.float32
            )
            upper, lower = outer[:channels, :channels], outer[channels:, channels:]
            sums_ref[a, 0] += weight * (upper + lower)
            sums_ref[a, 1] += top * upper + low * lower
            sums_ref[a, 2] += sine * (outer[channels:, :channels] - outer[:channels, channels:])

    def work(pair, carry):
        chosen = [pair * CHAINS + chain for chain in range(CHAINS)]
        for chain in range(CHAINS):
            prepare(chain, chosen[chain])
        for step in range(APPLICATIONS):
            for chain in range(CHAINS):
                moved, x_new, t_new = apply(chain, chosen[chain], step)
                if step < APPLICATIONS - 1:
                    store_held(
                        chain, (step + 1) % 2, 0, jnp.concatenate([x_new, t_new], axis=1)
                    )
                else:
                    finish(chain, chosen[chain], moved, x_new, t_new)
        return carry

    lax.fori_loop(0, slots // CHAINS, work, 0)

    def correlation(a, b):
        if b == 1:
            return sums_ref[a, 0]
        if b == 2:
            return sums_ref[a, 1] - sums_ref[a, 2]
        return sums_ref[a, 1] + sums_ref[a, 2]

    for place, (a, b) in enumerate(((1, 1), (1, 2), (2, 0), (2, 1), (2, 2))):
        grad_ref[place] = scale * (correlation(a, b) - correlation(2 - a, 2 - b).T)


def inverse_kernel(x_ref, dev_ref, high_ref, low_ref, out_ref):
    number, side, _, channels = x_ref.shape

    def transform(pair, carry):
        rows = jnp.concatenate(
            [dev_ref[2 * pair + j].reshape(side * number, channels) for j in range(2)], axis=1
        )
        high = rows.astype(jnp.bfloat16)
        low = (rows - high.astype(jnp.float32)).astype(jnp.bfloat16)
        result = dot(high_ref[...], high) + dot(low_ref[...], high) + dot(high_ref[...], low)
        for j in range(2):
            h = 2 * pair + j
            piece = result[:, j * channels : (j + 1) * channels]
            piece = piece.reshape(number, side, channels) + x_ref[:, h].astype(jnp.float32)
            out_ref[:, h] = piece.astype(jnp.bfloat16)
        return carry

    lax.fori_loop(0, side // 2, transform, 0, unroll=2)


def mirror_kernel(sum_ref, grad_ref):
    for place, (a, b) in enumerate(((1, 1), (1, 2), (2, 0), (2, 1), (2, 2))):
        piece = sum_ref[place]
        grad_ref[a, b] = piece
        if place:
            grad_ref[2 - a, 2 - b] = -piece.T


def whole(memory_space=pltpu.VMEM):
    return pl.BlockSpec(memory_space=memory_space)


def device_sum(partial):
    count = lax.axis_size("sample") * lax.axis_size("freq")
    rows = partial.reshape(-1, partial.shape[-1])
    share = -(-rows.shape[0] // count)
    padded = jnp.pad(rows, ((0, share * count - rows.shape[0]), (0, 0)))
    terms = lax.all_to_all(
        padded.reshape(count, share, -1), AXES, split_axis=0, concat_axis=0, tiled=True
    )
    own = jnp.sum(terms, axis=0, keepdims=True)
    shares = lax.all_to_all(
        jnp.broadcast_to(own, terms.shape), AXES, split_axis=0, concat_axis=0, tiled=True
    )
    return shares.reshape(padded.shape)[: rows.shape[0]].reshape(partial.shape)


def per_device(images, cotangent, kernel):
    number, side, _, channels = images.shape
    slots = side // 2
    wide = 2 * channels
    total = number * lax.axis_size("sample") * lax.axis_size("freq")
    forward_high, forward_low = split_table(forward_table(number, side))
    inverse_high, inverse_low = split_table(inverse_table(number, side))
    rows = side * 2 * number
    params = pltpu.CompilerParams(vmem_limit_bytes=VMEM_LIMIT)
    deviation, partial = pl.pallas_call(
        functools.partial(main_kernel, 2.0 / total),
        out_shape=(
            jax.ShapeDtypeStruct((side, side, number, channels), jnp.float32),
            jax.ShapeDtypeStruct((5, channels, channels), jnp.float32),
        ),
        in_specs=[whole(pltpu.SMEM)] + [whole()] * 5,
        out_specs=(whole(), whole()),
        scratch_shapes=[
            pltpu.VMEM((slots, side, 2 * number, wide), jnp.float32),
            pltpu.VMEM((CHAINS, 2, side + 2, 2 * number, wide), jnp.bfloat16),
            pltpu.VMEM((CHAINS, 3 * wide, wide), jnp.bfloat16),
            pltpu.VMEM((3, 3, channels, channels), jnp.float32),
            pltpu.VMEM((3, 3, channels, channels), jnp.float32),
        ],
        compiler_params=params,
        cost_estimate=pl.CostEstimate(
            flops=2 * APPLICATIONS * slots * rows * 3 * wide * wide,
            bytes_accessed=12 * 1024 * 1024,
            transcendentals=0,
        ),
        name="horner_and_gradient",
    )(jnp.asarray(slot_factors(side)), images, cotangent, kernel, jnp.asarray(forward_high), jnp.asarray(forward_low))
    summed = device_sum(partial)
    outputs = pl.pallas_call(
        inverse_kernel,
        out_shape=jax.ShapeDtypeStruct(images.shape, jnp.bfloat16),
        in_specs=[whole()] * 4,
        out_specs=whole(),
        compiler_params=params,
        cost_estimate=pl.CostEstimate(
            flops=6 * side * side * number * side * number * channels,
            bytes_accessed=8 * 1024 * 1024,
            transcendentals=0,
        ),
        name="inverse_transform",
    )(images, deviation, jnp.asarray(inverse_high), jnp.asarray(inverse_low))
    kernel_grad = pl.pallas_call(
        mirror_kernel,
        out_shape=jax.ShapeDtypeStruct(kernel.shape, jnp.float32),
        in_specs=[whole()],
        out_specs=whole(),
        name="mirror_taps",
    )(summed)
    return (outputs, kernel_grad)


def solution(mesh):
    split = P(AXES, None, None, None)
    return jax.shard_map(
        per_device,
        mesh=mesh,
        in_specs=(split, split, P()),
        out_specs=(split, P()),
        check_vma=False,
    )
```

time: 624 us -> 85.2 us (0.14); the launches traced: 616 us -> 84.9 us
  matrix products: 231 us -> 0 us
  waiting for transfers between devices: 195 us -> 6.32 us
  local copies, waits for them, and re-layouts: 94.3 us -> 2.51 us
  other arithmetic: 62.4 us -> 0.04 us
  Pallas kernels: 0 us -> 52.1 us
  blocking collectives: 0 us -> 20.6 us
  starting transfers between devices: 18.2 us -> 2.6 us
  between operations: 14.9 us -> 0.65 us
    dot_general x36 -> x0, matrix products: 231 us -> none  [the longest x8 94.6 us: full_multiply(): return jnp.einsum('fij,fjk->fik', former, latter, precision=HIGHEST)]
    psum x2 -> x0, waiting for transfers between devices: 147 us -> none  [the longest x1 85.8 us: per_device(): spec_grad = lax.psum((grad_real, grad_imag), 'sample')]
    pallas_call x0 -> x3, Pallas kernels: none -> 52.1 us  [the longest x1 43 us: per_device(): pl.pallas_call(functools.partial(main_kernel, 2.0 / total), out_shape=(ja...]
    all_to_all x3 -> x1, waiting for transfers between devices: 48.1 us -> 6.32 us  [device_sum(): lax.all_to_all(jnp.broadcast_to(own, terms.shape), AXES, split_axis=0, co...]
    neg x5 -> x0, other arithmetic: 27 us -> none  [the longest x1 14.9 us: adjoint(): return (jnp.swapaxes(matrix[0], 1, 2), -jnp.swapaxes(matrix[1], 1, 2))]
    neg x4 -> x0, local copies, waits for them, and re-layouts: 23.7 us -> none  [the longest x1 6.09 us: skew_gradient(): -(partial_term[1] + outer_term[1])]
    all_to_all x0 -> x1, blocking collectives: none -> 20.6 us  [device_sum(): lax.all_to_all(padded.reshape(count, share, -1), AXES, split_axis=0, conc...]
    convert_element_type x4 -> x0, local copies, waits for them, and re-layouts: 18.3 us -> none  [forward_spectrum(): spectrum.reshape(number, side_cells, half_cells, 2 * channels)]
  transfers between devices with their start and end apart: 5 -> 1, of which waited for: 4 -> 1; matrix products, arithmetic and copies ran while one was open for 36% -> 0% of each run, Pallas kernels for 0% -> 9%
where the time goes in v1:
time: 85.2 us; the launch traced here: 84.9 us
  Pallas kernels  52.1 us (61%)
  blocking collectives  20.6 us (24%)
  waiting for transfers between devices  6.32 us (7%)
  starting transfers between devices  2.6 us (3%)
  local copies, waits for them, and re-layouts  2.51 us (3%)
    pallas_call x1, Pallas kernels, per_device(): pl.pallas_call(functools.partial(main_kernel, 2.0 / total), out_shape=(ja...  43 us
    all_to_all x1, blocking collectives, device_sum(): lax.all_to_all(padded.reshape(count, share, -1), AXES, split_axis=0, conc...  20.6 us
    pallas_call x1, Pallas kernels, per_device(): pl.pallas_call(inverse_kernel, out_shape=jax.ShapeDtypeStruct(images.shap...  7.23 us
    all_to_all x1, waiting for transfers between devices, device_sum(): lax.all_to_all(jnp.broadcast_to(own, terms.shape), AXES, split_axis=0, co...  6.32 us
    all_to_all x1, starting transfers between devices, device_sum(): lax.all_to_all(jnp.broadcast_to(own, terms.shape), AXES, split_axis=0, co...  2.6 us
    pallas_call x1, Pallas kernels, per_device(): pl.pallas_call(mirror_kernel, out_shape=jax.ShapeDtypeStruct(kernel.shape...  1.92 us
  transfers between devices with their start and end apart: 1, of which 1 were waited for; matrix products, arithmetic and copies ran while one was open for 0% of the time, Pallas kernels for 9%

profile of v1, /device:TPU:0, one launch (start us, length us, event | category | flops | bytes accessed | tf_op | source)
XLA Modules:
  0.0 84.9 jit_solution(10614528212618498434)
XLA Ops:
  0.6 43.0 %horner_and_gradient.1 = (f32[32,32,8,128]{3,2,1,0:T(8,128)}, f32[5,128,128]{2,1,0:T(8,128)}) custom-call(f32[16,7]{1,0:T(8,128)} %constant.5.clone.factor_ref, bf16[8,32,32,128]{3,2,1,0:T(8,128)(2,1)} %x_ref.3, bf16[8,32,32,128]{3,2,1,0:T(8,128)(2,1)} %t_ref.1, f32[3,3,128,128]{3,2,1,0:T(8,128)} %kernel_ref.1, bf16[256,256]{1,0:T(8,128)(2,1)} %constant.14.clone.high_ref, ...), custom_call_target="tpu_custom_call" | custom-call | flops 22548578304 | bytes 12582912 | tf_op jit(solution)/shard_map/horner_and_gradient/pallas_call | solution.py:254
  43.6 1.0 %reshape.10 = f32[32,20,128]{2,1,0:T(8,128)S(1)} reshape(f32[5,128,128]{2,1,0:T(8,128)} %get-tuple-element.5) | data formatting | bytes 655360 | tf_op jit(solution)/shard_map/reshape | solution.py:236
  44.6 20.6 %all_to_all.10 = f32[32,20,128]{2,1,0:T(8,128)S(1)} all-to-all(f32[32,20,128]{2,1,0:T(8,128)S(1)} %reshape.10), channel_id=1, replica_groups=mesh['sample'=4,'freq'=8] {'sample','freq'}, dimensions={0} | all-to-all | bytes 655360 | tf_op jit(solution)/shard_map/all_to_all | solution.py:235
  65.3 0.8 broadcast_in_dim.2
  66.1 2.6 %all-to-all-start.1 = ((f32[32,20,128]{2,1,0:T(8,128)}), f32[32,20,128]{2,1,0:T(8,128)S(1)}, u32[]{:S(2)}, u32[]{:S(2)}) async-start(f32[32,20,128]{2,1,0:T(8,128)} %broadcast_in_dim.2), calls=%async_computation.1 | async-start | bytes 786432 | tf_op jit(solution)/shard_map/all_to_all | solution.py:239
  68.7 7.2 %inverse_transform.1 = bf16[8,32,32,128]{3,2,1,0:T(8,128)(2,1)} custom-call(bf16[8,32,32,128]{3,2,1,0:T(8,128)(2,1)} %x_ref.3, f32[32,32,8,128]{3,2,1,0:T(8,128)} %get-tuple-element.4.dev_ref, bf16[256,256]{1,0:T(8,128)(2,1)} %constant.16.clone.high_ref, bf16[256,256]{1,0:T(8,128)(2,1)} %constant.17.clone.low_ref), custom_call_target="tpu_custom_call" | custom-call | flops 1610612736 | bytes 8388608 | tf_op jit(solution)/shard_map/inverse_transform/pallas_call | solution.py:278
  75.9 6.3 %all-to-all-done.1 = f32[32,20,128]{2,1,0:T(8,128)S(1)} async-done(((f32[32,20,128]{2,1,0:T(8,128)}), f32[32,20,128]{2,1,0:T(8,128)S(1)}, u32[]{:S(2)}, u32[]{:S(2)}) %all-to-all-start.1) | async-done | bytes 327712 | tf_op jit(solution)/shard_map/all_to_all | solution.py:239
  82.2 0.7 reshape_reshape.3.sum_ref
  83.0 1.9 %mirror_taps.1 = f32[3,3,128,128]{3,2,1,0:T(8,128)} custom-call(f32[5,128,128]{2,1,0:T(8,128)} %reshape_reshape.3.sum_ref), custom_call_target="tpu_custom_call" | custom-call | tf_op jit(solution)/shard_map/mirror_taps/pallas_call | solution.py:291
  (1 shorter events, 0.0 us)
Async XLA Ops:
  66.1 16.1 %all-to-all-start.1 = ((f32[32,20,128]{2,1,0:T(8,128)}), f32[32,20,128]{2,1,0:T(8,128)S(1)}, u32[]{:S(2)}, u32[]{:S(2)}) async-start(f32[32,20,128]{2,1,0:T(8,128)} %broadcast_in_dim.2), calls=%async_computation.1 | async-start | bytes 786432 | tf_op jit(solution)/shard_map/all_to_all | solution.py:239

commit v2 on v1

v2 whole, which is shorter than its diff:
```python
import functools
import math

import jax
import jax.numpy as jnp
import numpy as np
from jax import lax
from jax.experimental import pallas as pl
from jax.experimental.pallas import tpu as pltpu
from jax.sharding import PartitionSpec as P

AXES = ("sample", "freq")
APPLICATIONS = 7
CHAINS = 2
IN_PARTS = 4
UNROLL = 4
GROUPS = 2
HALF_TAPS = ((1, 1), (1, 2), (2, 0), (2, 1), (2, 2))
VMEM_LIMIT = 56 * 1024 * 1024


def split_table(table):
    high = table.astype(jnp.bfloat16)
    low = (table - high.astype(np.float64)).astype(jnp.bfloat16)
    return high, low


def forward_table(number, side):
    place = np.arange(side)
    table = np.zeros((side, side))
    table[0] = 1.0
    table[1] = np.cos(np.pi * place)
    for slot in range(1, side // 2):
        angle = 2.0 * math.pi * ((slot * place) % side) / side
        table[2 * slot] = np.cos(angle)
        table[2 * slot + 1] = -np.sin(angle)
    full = np.einsum("kw,nm->knmw", table, np.eye(number))
    return full.reshape(side * number, number * side)


def inverse_table(number, side):
    place = np.arange(side)
    table = np.zeros((side, side))
    table[:, 0] = 2.0 / side
    table[:, 1] = 2.0 / side * np.cos(np.pi * place)
    for slot in range(1, side // 2):
        angle = 2.0 * math.pi * ((slot * place) % side) / side
        table[:, 2 * slot] = 4.0 / side * np.cos(angle)
        table[:, 2 * slot + 1] = -4.0 / side * np.sin(angle)
    full = np.einsum("wk,nm->nwkm", table, np.eye(number))
    return full.reshape(number * side, side * number)


def slot_factors(side):
    rows = [[1.0, -1.0, 0.0, 1.0 / side]]
    for slot in range(1, side // 2):
        angle = 2.0 * math.pi * slot / side
        rows.append([math.cos(angle), math.cos(angle), math.sin(angle), 2.0 / side])
    table = np.array(rows)
    weighted = table[:, :3] * table[:, 3:]
    return np.concatenate([table, weighted], axis=1).astype(np.float32)


def dot(left, right):
    return jnp.dot(left, right, preferred_element_type=jnp.float32)


def main_kernel(
    scale,
    factor_ref,
    x_hbm,
    t_hbm,
    kernel_ref,
    high_ref,
    low_ref,
    dev_hbm,
    grad_ref,
    x_ref,
    t_ref,
    base_ref,
    held_ref,
    weight_ref,
    taps_ref,
    sums_ref,
    dev_ref,
    left_ref,
    right_ref,
    in_sems,
    out_sems,
):
    number, side, _, channels = x_ref.shape
    slots = side // 2
    wide = 2 * channels
    part = side // IN_PARTS

    def incoming(index, place):
        source, target = ((x_hbm, x_ref), (t_hbm, t_ref))[index]
        rows = pl.ds(place * part, part)
        return pltpu.make_async_copy(
            source.at[:, rows], target.at[:, rows], in_sems.at[index, place]
        )

    def outgoing(slot):
        return pltpu.make_async_copy(dev_ref.at[slot], dev_hbm.at[slot], out_sems.at[slot])

    for place in range(IN_PARTS):
        for index in range(2):
            incoming(index, place).start()

    for a in range(3):
        flipped = [kernel_ref[a, b].T - kernel_ref[2 - a, 2 - b] for b in range(3)]
        taps_ref[a, 0] = -flipped[1]
        taps_ref[a, 1] = -(flipped[2] + flipped[0])
        taps_ref[a, 2] = flipped[2] - flipped[0]
    sums_ref[...] = jnp.zeros_like(sums_ref)
    left_ref[...] = jnp.zeros_like(left_ref)
    right_ref[...] = jnp.zeros_like(right_ref)

    def transform(h, carry):
        rows = jnp.concatenate(
            [
                x_ref[:, h].reshape(number * side, channels),
                t_ref[:, h].reshape(number * side, channels),
            ],
            axis=1,
        )
        result = dot(high_ref[...], rows) + dot(low_ref[...], rows)
        result = result.reshape(slots, 2, number, wide)
        base_ref[:, h, :number, :channels] = result[:, 0, :, :channels]
        base_ref[:, h, :number, channels:] = result[:, 1, :, :channels]
        base_ref[:, h, number:, :channels] = result[:, 0, :, channels:]
        base_ref[:, h, number:, channels:] = result[:, 1, :, channels:]
        return carry

    def store_held(chain, parity, rows):
        held = rows.astype(jnp.bfloat16)
        held_ref[chain, parity, 1 : 1 + side] = held
        held_ref[chain, parity, side + 1] = held[0]
        held_ref[chain, parity, 0] = held[side - 1]

    def prepare_taps(buffer, slot, a):
        cos_top, cos_low, sine = (factor_ref[slot, j] for j in range(3))
        first, second = taps_ref[a, 0], taps_ref[a, 1]
        cross = (sine * taps_ref[a, 2]).astype(jnp.bfloat16)
        row = a * wide
        middle, last = row + channels, row + wide
        weight_ref[buffer, row:middle, :channels] = (first + cos_top * second).astype(jnp.bfloat16)
        weight_ref[buffer, middle:last, channels:] = (first + cos_low * second).astype(jnp.bfloat16)
        weight_ref[buffer, row:middle, channels:] = cross
        weight_ref[buffer, middle:last, :channels] = -cross

    def apply(buffer, chain, parity, slot, step):
        left = jnp.concatenate(
            [
                held_ref[chain, parity, 2 - a : 2 - a + side].reshape(side * 2 * number, wide)
                for a in range(3)
            ],
            axis=1,
        )
        moved = dot(left, weight_ref[buffer]).reshape(side, 2 * number, wide)
        base = base_ref[slot]
        x_new = base[:, :number] + moved[:, :number]
        if step % 2 == 0:
            t_new = moved[:, number:] - base[:, number:]
        else:
            t_new = moved[:, number:] + base[:, number:]
        return moved, x_new, t_new

    def finish(buffer, slot, moved, x_new, t_new):
        dev_ref[slot, :, 0] = moved[:, :number, :channels]
        dev_ref[slot, :, 1] = moved[:, :number, channels:]
        left_ref[buffer] = t_new.reshape(side * number, wide).astype(jnp.bfloat16)
        around = jnp.concatenate([x_new[side - 1 :], x_new, x_new[:1]], axis=0)
        for a in range(3):
            right = around[2 - a : 2 - a + side].reshape(side * number, wide)
            right_ref[buffer, :, a * wide : (a + 1) * wide] = right.astype(jnp.bfloat16)

    def products(buffer, slot):
        weight, top, low, sine = (factor_ref[slot, j] for j in range(3, 7))
        outer_all = lax.dot_general(
            left_ref[buffer],
            right_ref[buffer],
            (((0,), (0,)), ((), ())),
            preferred_element_type=jnp.float32,
        )
        for a in range(3):
            outer = outer_all[:, a * wide : (a + 1) * wide]
            upper, lower = outer[:channels, :channels], outer[channels:, channels:]
            sums_ref[a, 0] += weight * (upper + lower)
            sums_ref[a, 1] += top * upper + low * lower
            sums_ref[a, 2] += sine * (outer[channels:, :channels] - outer[:channels, channels:])

    def work(group, odd):
        here, first = (CHAINS, 1) if odd else (0, 0)
        there = CHAINS - here
        before = jnp.maximum((group - 1) * CHAINS, 0)
        after = jnp.minimum((group + 1) * CHAINS, slots - CHAINS)
        jobs = [
            functools.partial(products, there + chain, before + chain) for chain in range(CHAINS)
        ] + [
            functools.partial(prepare_taps, there + chain, after + chain, a)
            for chain in range(CHAINS)
            for a in range(3)
        ]
        share = -(-len(jobs) // ((APPLICATIONS - 1) * CHAINS))
        for step in range(APPLICATIONS):
            for chain in range(CHAINS):
                slot = group * CHAINS + chain
                result = apply(here + chain, chain, (first + step) % 2, slot, step)
                if step < APPLICATIONS - 1:
                    store_held(
                        chain, (first + step + 1) % 2, jnp.concatenate(result[1:], axis=1)
                    )
                else:
                    finish(here + chain, slot, *result)
                if step == APPLICATIONS - 2:
                    store_held(chain, 1 - first, base_ref[after + chain])
                for job in jobs[:share]:
                    job()
                jobs = jobs[share:]

    for place in range(IN_PARTS):
        for index in range(2):
            incoming(index, place).wait()
        lax.fori_loop(place * part, (place + 1) * part, transform, 0, unroll=UNROLL)
    for chain in range(CHAINS):
        for a in range(3):
            prepare_taps(chain, chain, a)
        store_held(chain, 0, base_ref[chain])

    def some_groups(index, carry):
        for member in range(GROUPS):
            work(GROUPS * index + member, member % 2 == 1)
        for slot in range(GROUPS * CHAINS):
            outgoing(index * GROUPS * CHAINS + slot).start()
        return carry

    lax.fori_loop(0, slots // (GROUPS * CHAINS), some_groups, 0)
    for chain in range(CHAINS):
        products(CHAINS + chain, slots - CHAINS + chain)

    def correlation(a, b):
        if b == 1:
            return sums_ref[a, 0]
        if b == 2:
            return sums_ref[a, 1] - sums_ref[a, 2]
        return sums_ref[a, 1] + sums_ref[a, 2]

    for place, (a, b) in enumerate(HALF_TAPS):
        piece = scale * (correlation(a, b) - correlation(2 - a, 2 - b).T)
        grad_ref[place * channels : (place + 1) * channels] = piece.astype(grad_ref.dtype)
    rows = len(HALF_TAPS) * channels
    if grad_ref.shape[0] > rows:
        grad_ref[rows:] = jnp.zeros((grad_ref.shape[0] - rows, channels), grad_ref.dtype)
    for slot in range(slots):
        outgoing(slot).wait()


def inverse_kernel(x_ref, dev_ref, high_ref, low_ref, out_ref):
    number, side, _, channels = x_ref.shape

    def transform(pair, carry):
        rows = jnp.concatenate(
            [dev_ref[:, 2 * pair + j].reshape(side * number, channels) for j in range(2)], axis=1
        )
        high = rows.astype(jnp.bfloat16)
        low = (rows - high.astype(jnp.float32)).astype(jnp.bfloat16)
        result = dot(high_ref[...], high) + dot(low_ref[...], high) + dot(high_ref[...], low)
        for j in range(2):
            h = 2 * pair + j
            piece = result[:, j * channels : (j + 1) * channels]
            piece = piece.reshape(number, side, channels) + x_ref[:, h].astype(jnp.float32)
            out_ref[:, h] = piece.astype(jnp.bfloat16)
        return carry

    lax.fori_loop(0, side // 2, transform, 0, unroll=2)


def mirror_kernel(sum_ref, grad_ref):
    channels = sum_ref.shape[1]
    for place, (a, b) in enumerate(HALF_TAPS):
        piece = sum_ref[place * channels : (place + 1) * channels].astype(jnp.float32)
        grad_ref[a, b] = piece
        if place:
            grad_ref[2 - a, 2 - b] = -piece.T


def whole(memory_space=pltpu.VMEM):
    return pl.BlockSpec(memory_space=memory_space)


def device_sum(partial, count):
    terms = lax.all_to_all(
        partial.reshape(count, -1, partial.shape[1]), AXES, split_axis=0, concat_axis=0, tiled=True
    )
    own = jnp.sum(terms.astype(jnp.float32), axis=0, keepdims=True).astype(partial.dtype)
    shares = lax.all_to_all(
        jnp.broadcast_to(own, terms.shape), AXES, split_axis=0, concat_axis=0, tiled=True
    )
    return shares.reshape(partial.shape)


def per_device(images, cotangent, kernel):
    number, side, _, channels = images.shape
    slots = side // 2
    wide = 2 * channels
    count = lax.axis_size("sample") * lax.axis_size("freq")
    share = -(-len(HALF_TAPS) * channels // (8 * count)) * 8
    forward_high, forward_low = split_table(forward_table(number, side))
    inverse_high, inverse_low = split_table(inverse_table(number, side))
    rows = side * 2 * number
    params = pltpu.CompilerParams(vmem_limit_bytes=VMEM_LIMIT)
    deviation, partial = pl.pallas_call(
        functools.partial(main_kernel, 2.0 / (number * count)),
        out_shape=(
            jax.ShapeDtypeStruct((slots, side, 2, number, channels), jnp.float32),
            jax.ShapeDtypeStruct((count * share, channels), jnp.bfloat16),
        ),
        in_specs=[whole(pltpu.SMEM), whole(pl.ANY), whole(pl.ANY)] + [whole()] * 3,
        out_specs=(whole(pl.ANY), whole()),
        scratch_shapes=[
            pltpu.VMEM(images.shape, jnp.bfloat16),
            pltpu.VMEM(images.shape, jnp.bfloat16),
            pltpu.VMEM((slots, side, 2 * number, wide), jnp.float32),
            pltpu.VMEM((CHAINS, 2, side + 2, 2 * number, wide), jnp.bfloat16),
            pltpu.VMEM((2 * CHAINS, 3 * wide, wide), jnp.bfloat16),
            pltpu.VMEM((3, 3, channels, channels), jnp.float32),
            pltpu.VMEM((3, 3, channels, channels), jnp.float32),
            pltpu.VMEM((slots, side, 2, number, channels), jnp.float32),
            pltpu.VMEM((2 * CHAINS, side * number, wide), jnp.bfloat16),
            pltpu.VMEM((2 * CHAINS, side * number, 3 * wide), jnp.bfloat16),
            pltpu.SemaphoreType.DMA((2, IN_PARTS)),
            pltpu.SemaphoreType.DMA((slots,)),
        ],
        compiler_params=params,
        cost_estimate=pl.CostEstimate(
            flops=2 * APPLICATIONS * slots * rows * 3 * wide * wide,
            bytes_accessed=12 * 1024 * 1024,
            transcendentals=0,
        ),
        name="horner_and_gradient",
    )(
        jnp.asarray(slot_factors(side)),
        images,
        cotangent,
        kernel,
        jnp.asarray(forward_high),
        jnp.asarray(forward_low),
    )
    summed = device_sum(partial, count)
    outputs = pl.pallas_call(
        inverse_kernel,
        out_shape=jax.ShapeDtypeStruct(images.shape, jnp.bfloat16),
        in_specs=[whole()] * 4,
        out_specs=whole(),
        compiler_params=params,
        cost_estimate=pl.CostEstimate(
            flops=6 * side * side * number * side * number * channels,
            bytes_accessed=8 * 1024 * 1024,
            transcendentals=0,
        ),
        name="inverse_transform",
    )(images, deviation, jnp.asarray(inverse_high), jnp.asarray(inverse_low))
    kernel_grad = pl.pallas_call(
        mirror_kernel,
        out_shape=jax.ShapeDtypeStruct(kernel.shape, jnp.float32),
        in_specs=[whole()],
        out_specs=whole(),
        name="mirror_taps",
    )(summed)
    return (outputs, kernel_grad)


def solution(mesh):
    split = P(AXES, None, None, None)
    return jax.shard_map(
        per_device,
        mesh=mesh,
        in_specs=(split, split, P()),
        out_specs=(split, P()),
        check_vma=False,
    )
```

time: 85.2 us -> 65.7 us (0.77)
  Pallas kernels: 52.1 us -> 43.1 us
  waiting for transfers between devices: 6.32 us -> 1.31 us
  blocking collectives: 20.6 us -> 15.9 us
  local copies, waits for them, and re-layouts: 2.51 us -> 1.37 us
    pallas_call x1, Pallas kernels: 43 us -> 34.1 us  [per_device(): pl.pallas_call(functools.partial(main_kernel, 2.0 / (number * count)), ou...]
    all_to_all x1, waiting for transfers between devices: 6.32 us -> 1.31 us  [device_sum(): lax.all_to_all(jnp.broadcast_to(own, terms.shape), AXES, split_axis=0, co...]
    all_to_all x1, blocking collectives: 20.6 us -> 15.9 us  [device_sum(): lax.all_to_all(partial.reshape(count, -1, partial.shape[1]), AXES, split_...]
    reshape x1 -> x0, local copies, waits for them, and re-layouts: 1 us -> none  [device_sum(): padded.reshape(count, share, -1)]
  transfers between devices with their start and end apart: 1 -> 1, of which waited for: 1 -> 1; matrix products, arithmetic and copies ran while one was open for 0% -> 0% of each run, Pallas kernels for 9% -> 11%
where the time goes in v2:
time: 65.7 us; the launch traced here: 65.4 us
  Pallas kernels  43.1 us (66%)
  blocking collectives  15.9 us (24%)
  starting transfers between devices  3.06 us (5%)
  local copies, waits for them, and re-layouts  1.37 us (2%)
  waiting for transfers between devices  1.31 us (2%)
    pallas_call x1, Pallas kernels, per_device(): pl.pallas_call(functools.partial(main_kernel, 2.0 / (number * count)), ou...  34.1 us
    all_to_all x1, blocking collectives, device_sum(): lax.all_to_all(partial.reshape(count, -1, partial.shape[1]), AXES, split_...  15.9 us
    pallas_call x1, Pallas kernels, per_device(): pl.pallas_call(inverse_kernel, out_shape=jax.ShapeDtypeStruct(images.shap...  7.23 us
    all_to_all x1, starting transfers between devices, device_sum(): lax.all_to_all(jnp.broadcast_to(own, terms.shape), AXES, split_axis=0, co...  3.06 us
    pallas_call x1, Pallas kernels, per_device(): pl.pallas_call(mirror_kernel, out_shape=jax.ShapeDtypeStruct(kernel.shape...  1.85 us
  transfers between devices with their start and end apart: 1, of which 1 were waited for; matrix products, arithmetic and copies ran while one was open for 0% of the time, Pallas kernels for 11%

profile of v2, /device:TPU:0, one launch (start us, length us, event | category | flops | bytes accessed | tf_op | source)
XLA Modules:
  0.0 65.4 jit_solution(4426764563427676627)
XLA Ops:
  0.6 34.1 %horner_and_gradient.1 = (f32[16,32,2,8,128]{4,3,2,1,0:T(8,128)}, bf16[768,128]{1,0:T(8,128)(2,1)}) custom-call(f32[16,7]{1,0:T(8,128)} %constant.13.clone.factor_ref, bf16[8,32,32,128]{3,2,1,0:T(8,128)(2,1)} %x_ref.1, bf16[8,32,32,128]{3,2,1,0:T(8,128)(2,1)} %t_hbm.1, f32[3,3,128,128]{3,2,1,0:T(8,128)} %kernel_ref.1, ...), custom_call_target="tpu_custom_call" | custom-call | flops 22548578304 | bytes 12582912 | tf_op jit(solution)/shard_map/horner_and_gradient/pallas_call | solution.py:313
  34.7 15.9 %all_to_all.10 = bf16[32,24,128]{2,1,0:T(8,128)(2,1)S(1)} all-to-all(bf16[32,24,128]{2,1,0:T(8,128)(2,1)} %bitcast.3), channel_id=1, replica_groups=mesh['sample'=4,'freq'=8] {'sample','freq'}, dimensions={0} | all-to-all | bytes 393216 | tf_op jit(solution)/shard_map/all_to_all | solution.py:293
  50.6 0.7 %broadcast_in_dim.2 = bf16[32,24,128]{2,1,0:T(8,128)(2,1)} broadcast(bf16[24,128]{1,0:T(8,128)(2,1)S(1)} %reduce_sum.12), dimensions={1,2} | broadcast | bytes 202752 | tf_op jit(solution)/shard_map/broadcast_in_dim | solution.py:298
  51.3 3.1 %all-to-all-start.1 = ((bf16[32,24,128]{2,1,0:T(8,128)(2,1)}), bf16[32,24,128]{2,1,0:T(8,128)(2,1)S(1)}, u32[]{:S(2)}, u32[]{:S(2)}) async-start(bf16[32,24,128]{2,1,0:T(8,128)(2,1)} %broadcast_in_dim.2), calls=%async_computation.1 | async-start | bytes 393216 | tf_op jit(solution)/shard_map/all_to_all | solution.py:297
  54.4 7.2 %inverse_transform.1 = bf16[8,32,32,128]{3,2,1,0:T(8,128)(2,1)} custom-call(bf16[8,32,32,128]{3,2,1,0:T(8,128)(2,1)} %x_ref.1, f32[16,32,2,8,128]{4,3,2,1,0:T(8,128)} %get-tuple-element.4.dev_ref, bf16[256,256]{1,0:T(8,128)(2,1)} %constant.16.clone.high_ref, bf16[256,256]{1,0:T(8,128)(2,1)} %constant.17.clone.low_ref), custom_call_target="tpu_custom_call" | custom-call | flops 1610612736 | bytes 8388608 | tf_op jit(solution)/shard_map/inverse_transform/pallas_call | solution.py:351
  61.6 1.3 %all-to-all-done.1 = bf16[32,24,128]{2,1,0:T(8,128)(2,1)S(1)} async-done(((bf16[32,24,128]{2,1,0:T(8,128)(2,1)}), bf16[32,24,128]{2,1,0:T(8,128)(2,1)S(1)}, u32[]{:S(2)}, u32[]{:S(2)}) %all-to-all-start.1) | async-done | bytes 196640 | tf_op jit(solution)/shard_map/all_to_all | solution.py:297
  62.9 0.0 copy-start
  62.9 0.7 %copy-done = bf16[32,24,128]{2,1,0:T(8,128)(2,1)} copy-done((bf16[32,24,128]{2,1,0:T(8,128)(2,1)}, bf16[32,24,128]{2,1,0:T(8,128)(2,1)S(1)}, u32[]{:S(2)}) %copy-start) | copy-done | bytes 196632
  63.6 1.8 %mirror_taps.1 = f32[3,3,128,128]{3,2,1,0:T(8,128)} custom-call(bf16[768,128]{1,0:T(8,128)(2,1)} %bitcast.2), custom_call_target="tpu_custom_call" | custom-call | tf_op jit(solution)/shard_map/mirror_taps/pallas_call | solution.py:364
  (1 shorter events, 0.0 us)
Async XLA Ops:
  51.3 11.6 %all-to-all-start.1 = ((bf16[32,24,128]{2,1,0:T(8,128)(2,1)}), bf16[32,24,128]{2,1,0:T(8,128)(2,1)S(1)}, u32[]{:S(2)}, u32[]{:S(2)}) async-start(bf16[32,24,128]{2,1,0:T(8,128)(2,1)} %broadcast_in_dim.2), calls=%async_computation.1 | async-start | bytes 393216 | tf_op jit(solution)/shard_map/all_to_all | solution.py:297
  62.9 0.7 %copy-start = (bf16[32,24,128]{2,1,0:T(8,128)(2,1)}, bf16[32,24,128]{2,1,0:T(8,128)(2,1)S(1)}, u32[]{:S(2)}) copy-start(bf16[32,24,128]{2,1,0:T(8,128)(2,1)S(1)} %all-to-all-done.1) | copy-start | bytes 589828

commit v3 on v2

--- a/solution.py
+++ b/solution.py
@@ -13,7 +13,8 @@
 APPLICATIONS = 7
 CHAINS = 2
 IN_PARTS = 4
-UNROLL = 4
+AHEAD = 2
+UNROLL = 8
 GROUPS = 2
 HALF_TAPS = ((1, 1), (1, 2), (2, 0), (2, 1), (2, 2))
 VMEM_LIMIT = 56 * 1024 * 1024
@@ -70,13 +71,14 @@
     factor_ref,
     x_hbm,
     t_hbm,
-    kernel_ref,
-    high_ref,
-    low_ref,
+    kernel_hbm,
+    table_hbm,
     dev_hbm,
     grad_ref,
     x_ref,
     t_ref,
+    kernel_ref,
+    table_ref,
     base_ref,
     held_ref,
     weight_ref,
@@ -86,11 +88,13 @@
     left_ref,
     right_ref,
     in_sems,
+    other_sems,
     out_sems,
 ):
     number, side, _, channels = x_ref.shape
     slots = side // 2
     wide = 2 * channels
+    pairs = side // 2
     part = side // IN_PARTS
 
     def incoming(index, place):
@@ -103,18 +107,28 @@
     def outgoing(slot):
         return pltpu.make_async_copy(dev_ref.at[slot], dev_hbm.at[slot], out_sems.at[slot])
 
-    for place in range(IN_PARTS):
+    table_copy = pltpu.make_async_copy(table_hbm, table_ref, other_sems.at[0])
+    kernel_copy = pltpu.make_async_copy(kernel_hbm, kernel_ref, other_sems.at[1])
+    table_copy.start()
+    for place in range(AHEAD):
         for index in range(2):
             incoming(index, place).start()
-
-    for a in range(3):
-        flipped = [kernel_ref[a, b].T - kernel_ref[2 - a, 2 - b] for b in range(3)]
-        taps_ref[a, 0] = -flipped[1]
-        taps_ref[a, 1] = -(flipped[2] + flipped[0])
-        taps_ref[a, 2] = flipped[2] - flipped[0]
+    kernel_copy.start()
     sums_ref[...] = jnp.zeros_like(sums_ref)
     left_ref[...] = jnp.zeros_like(left_ref)
     right_ref[...] = jnp.zeros_like(right_ref)
+
+    def make_taps():
+        for a in range(3):
+            flipped = [kernel_ref[a, b].T - kernel_ref[2 - a, 2 - b] for b in range(3)]
+            place = 3 - 3 * a // 2 if a != 1 else 1
+            taps_ref[place, 0] = -flipped[1]
+            taps_ref[place, 1] = -(flipped[2] + flipped[0])
+            taps_ref[place, 2] = flipped[2] - flipped[0]
+        outside = 0.5 * (taps_ref[0] + taps_ref[3])
+        inside = 0.5 * taps_ref[1]
+        taps_ref[1] = outside + inside
+        taps_ref[2] = outside - inside
 
     def transform(h, carry):
         rows = jnp.concatenate(
@@ -124,56 +138,67 @@
             ],
             axis=1,
         )
-        result = dot(high_ref[...], rows) + dot(low_ref[...], rows)
-        result = result.reshape(slots, 2, number, wide)
-        base_ref[:, h, :number, :channels] = result[:, 0, :, :channels]
-        base_ref[:, h, :number, channels:] = result[:, 1, :, :channels]
-        base_ref[:, h, number:, :channels] = result[:, 0, :, channels:]
-        base_ref[:, h, number:, channels:] = result[:, 1, :, channels:]
+        both = dot(table_ref[...], rows)
+        half = side * number
+        result = (both[:half] + both[half:]).reshape(slots, 2, number, wide)
+        pair, odd = h // 2, h % 2
+        base_ref[:, odd, pair, :number, :channels] = result[:, 0, :, :channels]
+        base_ref[:, odd, pair, :number, channels:] = result[:, 1, :, :channels]
+        base_ref[:, odd, pair, number:, :channels] = result[:, 0, :, channels:]
+        base_ref[:, odd, pair, number:, channels:] = result[:, 1, :, channels:]
         return carry
 
-    def store_held(chain, parity, rows):
-        held = rows.astype(jnp.bfloat16)
-        held_ref[chain, parity, 1 : 1 + side] = held
-        held_ref[chain, parity, side + 1] = held[0]
-        held_ref[chain, parity, 0] = held[side - 1]
+    def before_of(rows):
+        return jnp.concatenate([rows[pairs - 1 :], rows[: pairs - 1]], axis=0)
+
+    def after_of(rows):
+        return jnp.concatenate([rows[1:], rows[:1]], axis=0)
+
+    def store_held(chain, parity, even, odd):
+        held_ref[chain, parity, 0] = (before_of(odd) - odd).astype(jnp.bfloat16)
+        held_ref[chain, parity, 1] = (even + odd).astype(jnp.bfloat16)
+        held_ref[chain, parity, 2] = (odd - even).astype(jnp.bfloat16)
+        held_ref[chain, parity, 3] = (even - after_of(even)).astype(jnp.bfloat16)
 
     def prepare_taps(buffer, slot, a):
         cos_top, cos_low, sine = (factor_ref[slot, j] for j in range(3))
         first, second = taps_ref[a, 0], taps_ref[a, 1]
         cross = (sine * taps_ref[a, 2]).astype(jnp.bfloat16)
-        row = a * wide
-        middle, last = row + channels, row + wide
-        weight_ref[buffer, row:middle, :channels] = (first + cos_top * second).astype(jnp.bfloat16)
-        weight_ref[buffer, middle:last, channels:] = (first + cos_low * second).astype(jnp.bfloat16)
-        weight_ref[buffer, row:middle, channels:] = cross
-        weight_ref[buffer, middle:last, :channels] = -cross
-
-    def apply(buffer, chain, parity, slot, step):
-        left = jnp.concatenate(
-            [
-                held_ref[chain, parity, 2 - a : 2 - a + side].reshape(side * 2 * number, wide)
-                for a in range(3)
-            ],
-            axis=1,
-        )
-        moved = dot(left, weight_ref[buffer]).reshape(side, 2 * number, wide)
-        base = base_ref[slot]
+        weight_ref[buffer, a, :channels, :channels] = (first + cos_top * second).astype(jnp.bfloat16)
+        weight_ref[buffer, a, channels:, channels:] = (first + cos_low * second).astype(jnp.bfloat16)
+        weight_ref[buffer, a, :channels, channels:] = cross
+        weight_ref[buffer, a, channels:, :channels] = -cross
+
+    def apply(buffer, chain, parity, slot):
+        def part(place):
+            left = held_ref[chain, parity, place].reshape(pairs * 2 * number, wide)
+            return dot(left, weight_ref[buffer, place]).reshape(pairs, 2 * number, wide)
+
+        first, inner, outer, last = (part(place) for place in range(4))
+        return first + (inner + outer), (inner - outer) - last
+
+    def advance(moved, base, step):
         x_new = base[:, :number] + moved[:, :number]
         if step % 2 == 0:
             t_new = moved[:, number:] - base[:, number:]
         else:
             t_new = moved[:, number:] + base[:, number:]
-        return moved, x_new, t_new
-
-    def finish(buffer, slot, moved, x_new, t_new):
-        dev_ref[slot, :, 0] = moved[:, :number, :channels]
-        dev_ref[slot, :, 1] = moved[:, :number, channels:]
-        left_ref[buffer] = t_new.reshape(side * number, wide).astype(jnp.bfloat16)
-        around = jnp.concatenate([x_new[side - 1 :], x_new, x_new[:1]], axis=0)
-        for a in range(3):
-            right = around[2 - a : 2 - a + side].reshape(side * number, wide)
-            right_ref[buffer, :, a * wide : (a + 1) * wide] = right.astype(jnp.bfloat16)
+        return x_new, t_new
+
+    def finish(buffer, slot, even, odd, even_new, odd_new):
+        for place, moved in enumerate((even, odd)):
+            dev_ref[slot, place, :, 0] = moved[:, :number, :channels]
+            dev_ref[slot, place, :, 1] = moved[:, :number, channels:]
+        half = pairs * number
+        even_x, even_t = even_new
+        odd_x, odd_t = odd_new
+        left_ref[buffer, :half] = even_t.reshape(half, wide).astype(jnp.bfloat16)
+        left_ref[buffer, half:] = odd_t.reshape(half, wide).astype(jnp.bfloat16)
+        shifted = ((odd_x, after_of(even_x)), (even_x, odd_x), (before_of(odd_x), even_x))
+        for a, (top, low) in enumerate(shifted):
+            columns = slice(a * wide, (a + 1) * wide)
+            right_ref[buffer, :half, columns] = top.reshape(half, wide).astype(jnp.bfloat16)
+            right_ref[buffer, half:, columns] = low.reshape(half, wide).astype(jnp.bfloat16)
 
     def products(buffer, slot):
         weight, top, low, sine = (factor_ref[slot, j] for j in range(3, 7))
@@ -200,33 +225,47 @@
         ] + [
             functools.partial(prepare_taps, there + chain, after + chain, a)
             for chain in range(CHAINS)
-            for a in range(3)
+            for a in range(4)
         ]
         share = -(-len(jobs) // ((APPLICATIONS - 1) * CHAINS))
         for step in range(APPLICATIONS):
             for chain in range(CHAINS):
                 slot = group * CHAINS + chain
-                result = apply(here + chain, chain, (first + step) % 2, slot, step)
+                even, odd = apply(here + chain, chain, (first + step) % 2, slot)
+                even_new = advance(even, base_ref[slot, 0], step)
+                odd_new = advance(odd, base_ref[slot, 1], step)
                 if step < APPLICATIONS - 1:
                     store_held(
-                        chain, (first + step + 1) % 2, jnp.concatenate(result[1:], axis=1)
+                        chain,
+                        (first + step + 1) % 2,
+                        jnp.concatenate(even_new, axis=1),
+                        jnp.concatenate(odd_new, axis=1),
                     )
                 else:
-                    finish(here + chain, slot, *result)
+                    finish(here + chain, slot, even, odd, even_new, odd_new)
                 if step == APPLICATIONS - 2:
-                    store_held(chain, 1 - first, base_ref[after + chain])
+                    store_held(
+                        chain, 1 - first, base_ref[after + chain, 0], base_ref[after + chain, 1]
+                    )
                 for job in jobs[:share]:
                     job()
                 jobs = jobs[share:]
 
+    table_copy.wait()
     for place in range(IN_PARTS):
         for index in range(2):
             incoming(index, place).wait()
+        if place + AHEAD < IN_PARTS:
+            for index in range(2):
+                incoming(index, place + AHEAD).start()
+        if place == 1:
+            kernel_copy.wait()
+            make_taps()
         lax.fori_loop(place * part, (place + 1) * part, transform, 0, unroll=UNROLL)
     for chain in range(CHAINS):
-        for a in range(3):
+        for a in range(4):
             prepare_taps(chain, chain, a)
-        store_held(chain, 0, base_ref[chain])
+        store_held(chain, 0, base_ref[chain, 0], base_ref[chain, 1])
 
     def some_groups(index, carry):
         for member in range(GROUPS):
@@ -261,7 +300,7 @@
 
     def transform(pair, carry):
         rows = jnp.concatenate(
-            [dev_ref[:, 2 * pair + j].reshape(side * number, channels) for j in range(2)], axis=1
+            [dev_ref[:, j, pair].reshape(side * number, channels) for j in range(2)], axis=1
         )
         high = rows.astype(jnp.bfloat16)
         low = (rows - high.astype(jnp.float32)).astype(jnp.bfloat16)
@@ -306,30 +345,33 @@
     wide = 2 * channels
     count = lax.axis_size("sample") * lax.axis_size("freq")
     share = -(-len(HALF_TAPS) * channels // (8 * count)) * 8
-    forward_high, forward_low = split_table(forward_table(number, side))
+    forward_both = np.concatenate(split_table(forward_table(number, side)), axis=0)
     inverse_high, inverse_low = split_table(inverse_table(number, side))
     rows = side * 2 * number
     params = pltpu.CompilerParams(vmem_limit_bytes=VMEM_LIMIT)
     deviation, partial = pl.pallas_call(
         functools.partial(main_kernel, 2.0 / (number * count)),
         out_shape=(
-            jax.ShapeDtypeStruct((slots, side, 2, number, channels), jnp.float32),
+            jax.ShapeDtypeStruct((slots, 2, side // 2, 2, number, channels), jnp.float32),
             jax.ShapeDtypeStruct((count * share, channels), jnp.bfloat16),
         ),
-        in_specs=[whole(pltpu.SMEM), whole(pl.ANY), whole(pl.ANY)] + [whole()] * 3,
+        in_specs=[whole(pltpu.SMEM)] + [whole(pl.ANY)] * 4,
         out_specs=(whole(pl.ANY), whole()),
         scratch_shapes=[
             pltpu.VMEM(images.shape, jnp.bfloat16),
             pltpu.VMEM(images.shape, jnp.bfloat16),
-            pltpu.VMEM((slots, side, 2 * number, wide), jnp.float32),
-            pltpu.VMEM((CHAINS, 2, side + 2, 2 * number, wide), jnp.bfloat16),
-            pltpu.VMEM((2 * CHAINS, 3 * wide, wide), jnp.bfloat16),
+            pltpu.VMEM(kernel.shape, jnp.float32),
+            pltpu.VMEM(forward_both.shape, jnp.bfloat16),
+            pltpu.VMEM((slots, 2, side // 2, 2 * number, wide), jnp.float32),
+            pltpu.VMEM((CHAINS, 2, 4, side // 2, 2 * number, wide), jnp.bfloat16),
+            pltpu.VMEM((2 * CHAINS, 4, wide, wide), jnp.bfloat16),
+            pltpu.VMEM((4, 3, channels, channels), jnp.float32),
             pltpu.VMEM((3, 3, channels, channels), jnp.float32),
-            pltpu.VMEM((3, 3, channels, channels), jnp.float32),
-            pltpu.VMEM((slots, side, 2, number, channels), jnp.float32),
+            pltpu.VMEM((slots, 2, side // 2, 2, number, channels), jnp.float32),
             pltpu.VMEM((2 * CHAINS, side * number, wide), jnp.bfloat16),
             pltpu.VMEM((2 * CHAINS, side * number, 3 * wide), jnp.bfloat16),
             pltpu.SemaphoreType.DMA((2, IN_PARTS)),
+            pltpu.SemaphoreType.DMA((2,)),
             pltpu.SemaphoreType.DMA((slots,)),
         ],
         compiler_params=params,
@@ -344,8 +386,7 @@
         images,
         cotangent,
         kernel,
-        jnp.asarray(forward_high),
-        jnp.asarray(forward_low),
+        jnp.asarray(forward_both),
     )
     summed = device_sum(partial, count)
     outputs = pl.pallas_call(

time: 65.7 us -> 61.1 us (0.930)
  Pallas kernels: 43.1 us -> 38.5 us
    pallas_call x1, Pallas kernels: 34.1 us -> 29.4 us  [per_device(): pl.pallas_call(functools.partial(main_kernel, 2.0 / (number * count)), ou...]
  transfers between devices with their start and end apart: 1 -> 1, of which waited for: 1 -> 1; matrix products, arithmetic and copies ran while one was open for 0% -> 0% of each run, Pallas kernels for 11% -> 12%
where the time goes in v3:
time: 61.1 us; the launch traced here: 60.8 us
  Pallas kernels  38.5 us (63%)
  blocking collectives  15.9 us (26%)
  starting transfers between devices  3.06 us (5%)
  local copies, waits for them, and re-layouts  1.37 us (2%)
  waiting for transfers between devices  1.31 us (2%)
  between operations  0.65 us (1%)
    pallas_call x1, Pallas kernels, per_device(): pl.pallas_call(functools.partial(main_kernel, 2.0 / (number * count)), ou...  29.4 us
    all_to_all x1, blocking collectives, device_sum(): lax.all_to_all(partial.reshape(count, -1, partial.shape[1]), AXES, split_...  15.9 us
    pallas_call x1, Pallas kernels, per_device(): pl.pallas_call(inverse_kernel, out_shape=jax.ShapeDtypeStruct(images.shap...  7.23 us
    all_to_all x1, starting transfers between devices, device_sum(): lax.all_to_all(jnp.broadcast_to(own, terms.shape), AXES, split_axis=0, co...  3.06 us
    pallas_call x1, Pallas kernels, per_device(): pl.pallas_call(mirror_kernel, out_shape=jax.ShapeDtypeStruct(kernel.shape...  1.85 us
    all_to_all x1, waiting for transfers between devices, device_sum(): lax.all_to_all(jnp.broadcast_to(own, terms.shape), AXES, split_axis=0, co...  1.31 us
  transfers between devices with their start and end apart: 1, of which 1 were waited for; matrix products, arithmetic and copies ran while one was open for 0% of the time, Pallas kernels for 12%

profile of v3, /device:TPU:0, one launch (start us, length us, event | category | flops | bytes accessed | tf_op | source)
XLA Modules:
  0.0 60.8 jit_solution(17372535181541949720)
XLA Ops:
  0.6 29.4 %horner_and_gradient.1 = (f32[16,2,16,2,8,128]{5,4,3,2,1,0:T(8,128)}, bf16[768,128]{1,0:T(8,128)(2,1)}) custom-call(f32[16,7]{1,0:T(8,128)} %constant.11.clone.factor_ref, bf16[8,32,32,128]{3,2,1,0:T(8,128)(2,1)} %x_ref.1, bf16[8,32,32,128]{3,2,1,0:T(8,128)(2,1)} %t_hbm.1, f32[3,3,128,128]{3,2,1,0:T(8,128)} %kernel_hbm.1, ...), custom_call_target="tpu_custom_call" | custom-call | flops 22548578304 | bytes 12582912 | tf_op jit(solution)/shard_map/horner_and_gradient/pallas_call | solution.py:352
  30.1 15.9 %all_to_all.10 = bf16[32,24,128]{2,1,0:T(8,128)(2,1)S(1)} all-to-all(bf16[32,24,128]{2,1,0:T(8,128)(2,1)} %bitcast.3), channel_id=1, replica_groups=mesh['sample'=4,'freq'=8] {'sample','freq'}, dimensions={0} | all-to-all | bytes 393216 | tf_op jit(solution)/shard_map/all_to_all | solution.py:332
  46.0 0.7 %broadcast_in_dim.2 = bf16[32,24,128]{2,1,0:T(8,128)(2,1)} broadcast(bf16[24,128]{1,0:T(8,128)(2,1)S(1)} %reduce_sum.12), dimensions={1,2} | broadcast | bytes 202752 | tf_op jit(solution)/shard_map/broadcast_in_dim | solution.py:337
  46.7 3.1 %all-to-all-start.1 = ((bf16[32,24,128]{2,1,0:T(8,128)(2,1)}), bf16[32,24,128]{2,1,0:T(8,128)(2,1)S(1)}, u32[]{:S(2)}, u32[]{:S(2)}) async-start(bf16[32,24,128]{2,1,0:T(8,128)(2,1)} %broadcast_in_dim.2), calls=%async_computation.1 | async-start | bytes 393216 | tf_op jit(solution)/shard_map/all_to_all | solution.py:336
  49.7 7.2 %inverse_transform.1 = bf16[8,32,32,128]{3,2,1,0:T(8,128)(2,1)} custom-call(bf16[8,32,32,128]{3,2,1,0:T(8,128)(2,1)} %x_ref.1, f32[16,2,16,2,8,128]{5,4,3,2,1,0:T(8,128)} %get-tuple-element.4.dev_ref, bf16[256,256]{1,0:T(8,128)(2,1)} %constant.13.clone.high_ref, bf16[256,256]{1,0:T(8,128)(2,1)} %constant.14.clone.low_ref), custom_call_target="tpu_custom_call" | custom-call | flops 1610612736 | bytes 8388608 | tf_op jit(solution)/shard_map/inverse_transform/pallas_call | solution.py:392
  57.0 1.3 %all-to-all-done.1 = bf16[32,24,128]{2,1,0:T(8,128)(2,1)S(1)} async-done(((bf16[32,24,128]{2,1,0:T(8,128)(2,1)}), bf16[32,24,128]{2,1,0:T(8,128)(2,1)S(1)}, u32[]{:S(2)}, u32[]{:S(2)}) %all-to-all-start.1) | async-done | bytes 196640 | tf_op jit(solution)/shard_map/all_to_all | solution.py:336
  58.3 0.0 copy-start
  58.3 0.7 %copy-done = bf16[32,24,128]{2,1,0:T(8,128)(2,1)} copy-done((bf16[32,24,128]{2,1,0:T(8,128)(2,1)}, bf16[32,24,128]{2,1,0:T(8,128)(2,1)S(1)}, u32[]{:S(2)}) %copy-start) | copy-done | bytes 196632
  59.0 1.8 %mirror_taps.1 = f32[3,3,128,128]{3,2,1,0:T(8,128)} custom-call(bf16[768,128]{1,0:T(8,128)(2,1)} %bitcast.2), custom_call_target="tpu_custom_call" | custom-call | tf_op jit(solution)/shard_map/mirror_taps/pallas_call | solution.py:405
  (1 shorter events, 0.0 us)
Async XLA Ops:
  46.7 11.6 %all-to-all-start.1 = ((bf16[32,24,128]{2,1,0:T(8,128)(2,1)}), bf16[32,24,128]{2,1,0:T(8,128)(2,1)S(1)}, u32[]{:S(2)}, u32[]{:S(2)}) async-start(bf16[32,24,128]{2,1,0:T(8,128)(2,1)} %broadcast_in_dim.2), calls=%async_computation.1 | async-start | bytes 393216 | tf_op jit(solution)/shard_map/all_to_all | solution.py:336
  58.3 0.7 %copy-start = (bf16[32,24,128]{2,1,0:T(8,128)(2,1)}, bf16[32,24,128]{2,1,0:T(8,128)(2,1)S(1)}, u32[]{:S(2)}) copy-start(bf16[32,24,128]{2,1,0:T(8,128)(2,1)S(1)} %all-to-all-done.1) | copy-start | bytes 589828

commit v4 on v3

--- a/solution.py
+++ b/solution.py
@@ -18,6 +18,7 @@
 GROUPS = 2
 HALF_TAPS = ((1, 1), (1, 2), (2, 0), (2, 1), (2, 2))
 VMEM_LIMIT = 56 * 1024 * 1024
+MIRROR_LIMIT = 4 * 1024 * 1024
 
 
 def split_table(table):
@@ -67,7 +68,6 @@
 
 
 def main_kernel(
-    scale,
     factor_ref,
     x_hbm,
     t_hbm,
@@ -155,10 +155,11 @@
         return jnp.concatenate([rows[1:], rows[:1]], axis=0)
 
     def store_held(chain, parity, even, odd):
-        held_ref[chain, parity, 0] = (before_of(odd) - odd).astype(jnp.bfloat16)
-        held_ref[chain, parity, 1] = (even + odd).astype(jnp.bfloat16)
-        held_ref[chain, parity, 2] = (odd - even).astype(jnp.bfloat16)
-        held_ref[chain, parity, 3] = (even - after_of(even)).astype(jnp.bfloat16)
+        even, odd = even.astype(jnp.bfloat16), odd.astype(jnp.bfloat16)
+        held_ref[chain, parity, 0] = before_of(odd) - odd
+        held_ref[chain, parity, 1] = even + odd
+        held_ref[chain, parity, 2] = odd - even
+        held_ref[chain, parity, 3] = even - after_of(even)
 
     def prepare_taps(buffer, slot, a):
         cos_top, cos_low, sine = (factor_ref[slot, j] for j in range(3))
@@ -261,10 +262,11 @@
         if place == 1:
             kernel_copy.wait()
             make_taps()
+            for chain in range(CHAINS):
+                for a in range(4):
+                    prepare_taps(chain, chain, a)
         lax.fori_loop(place * part, (place + 1) * part, transform, 0, unroll=UNROLL)
     for chain in range(CHAINS):
-        for a in range(4):
-            prepare_taps(chain, chain, a)
         store_held(chain, 0, base_ref[chain, 0], base_ref[chain, 1])
 
     def some_groups(index, carry):
@@ -286,7 +288,7 @@
         return sums_ref[a, 1] + sums_ref[a, 2]
 
     for place, (a, b) in enumerate(HALF_TAPS):
-        piece = scale * (correlation(a, b) - correlation(2 - a, 2 - b).T)
+        piece = correlation(a, b) - correlation(2 - a, 2 - b).T
         grad_ref[place * channels : (place + 1) * channels] = piece.astype(grad_ref.dtype)
     rows = len(HALF_TAPS) * channels
     if grad_ref.shape[0] > rows:
@@ -328,11 +330,10 @@
     return pl.BlockSpec(memory_space=memory_space)
 
 
-def device_sum(partial, count):
-    terms = lax.all_to_all(
-        partial.reshape(count, -1, partial.shape[1]), AXES, split_axis=0, concat_axis=0, tiled=True
-    )
-    own = jnp.sum(terms.astype(jnp.float32), axis=0, keepdims=True).astype(partial.dtype)
+def device_sum(partial, scale, count):
+    pieces = partial.reshape(count, -1, 2, partial.shape[1])
+    terms = lax.all_to_all(pieces, AXES, split_axis=0, concat_axis=0, tiled=True)
+    own = jnp.sum(scale * terms.astype(jnp.float32), axis=0, keepdims=True).astype(partial.dtype)
     shares = lax.all_to_all(
         jnp.broadcast_to(own, terms.shape), AXES, split_axis=0, concat_axis=0, tiled=True
     )
@@ -344,13 +345,13 @@
     slots = side // 2
     wide = 2 * channels
     count = lax.axis_size("sample") * lax.axis_size("freq")
-    share = -(-len(HALF_TAPS) * channels // (8 * count)) * 8
+    share = -(-len(HALF_TAPS) * channels // (2 * count)) * 2
     forward_both = np.concatenate(split_table(forward_table(number, side)), axis=0)
     inverse_high, inverse_low = split_table(inverse_table(number, side))
     rows = side * 2 * number
     params = pltpu.CompilerParams(vmem_limit_bytes=VMEM_LIMIT)
     deviation, partial = pl.pallas_call(
-        functools.partial(main_kernel, 2.0 / (number * count)),
+        main_kernel,
         out_shape=(
             jax.ShapeDtypeStruct((slots, 2, side // 2, 2, number, channels), jnp.float32),
             jax.ShapeDtypeStruct((count * share, channels), jnp.bfloat16),
@@ -388,7 +389,7 @@
         kernel,
         jnp.asarray(forward_both),
     )
-    summed = device_sum(partial, count)
+    summed = device_sum(partial, 2.0 / (number * count), count)
     outputs = pl.pallas_call(
         inverse_kernel,
         out_shape=jax.ShapeDtypeStruct(images.shape, jnp.bfloat16),
@@ -407,6 +408,7 @@
         out_shape=jax.ShapeDtypeStruct(kernel.shape, jnp.float32),
         in_specs=[whole()],
         out_specs=whole(),
+        compiler_params=pltpu.CompilerParams(vmem_limit_bytes=MIRROR_LIMIT),
         name="mirror_taps",
     )(summed)
     return (outputs, kernel_grad)

time: 61.1 us -> 57.1 us (0.935)
  Pallas kernels: 38.5 us -> 36.3 us
  blocking collectives: 15.9 us -> 15.2 us
  local copies, waits for them, and re-layouts: 1.37 us -> 0.75 us
  waiting for transfers between devices: 1.31 us -> 0.69 us
    pallas_call x1, Pallas kernels: 29.4 us -> 28.2 us  [per_device(): pl.pallas_call(main_kernel, out_shape=(jax.ShapeDtypeStruct((slots, 2, si...]
    pallas_call x1, Pallas kernels: 1.85 us -> 0.92 us  [per_device(): pl.pallas_call(mirror_kernel, out_shape=jax.ShapeDtypeStruct(kernel.shape...]
    unnamed x2 -> x0, local copies, waits for them, and re-layouts: 0.66 us -> none
    all_to_all x1, blocking collectives: 15.9 us -> 15.2 us  [device_sum(): lax.all_to_all(pieces, AXES, split_axis=0, concat_axis=0, tiled=True)]
    all_to_all x1, waiting for transfers between devices: 1.31 us -> 0.69 us  [device_sum(): lax.all_to_all(jnp.broadcast_to(own, terms.shape), AXES, split_axis=0, co...]
  transfers between devices with their start and end apart: 1 -> 1, of which waited for: 1 -> 1; matrix products, arithmetic and copies ran while one was open for 0% -> 0% of each run, Pallas kernels for 12% -> 13%
where the time goes in v4:
time: 57.1 us; the launch traced here: 56.8 us
  Pallas kernels  36.3 us (64%)
  blocking collectives  15.2 us (27%)
  starting transfers between devices  2.98 us (5%)
  local copies, waits for them, and re-layouts  0.75 us (1%)
  waiting for transfers between devices  0.69 us (1%)
  between operations  0.65 us (1%)
    pallas_call x1, Pallas kernels, per_device(): pl.pallas_call(main_kernel, out_shape=(jax.ShapeDtypeStruct((slots, 2, si...  28.2 us
    all_to_all x1, blocking collectives, device_sum(): lax.all_to_all(pieces, AXES, split_axis=0, concat_axis=0, tiled=True)  15.2 us
    pallas_call x1, Pallas kernels, per_device(): pl.pallas_call(inverse_kernel, out_shape=jax.ShapeDtypeStruct(images.shap...  7.23 us
    all_to_all x1, starting transfers between devices, device_sum(): lax.all_to_all(jnp.broadcast_to(own, terms.shape), AXES, split_axis=0, co...  2.98 us
  transfers between devices with their start and end apart: 1, of which 1 were waited for; matrix products, arithmetic and copies ran while one was open for 0% of the time, Pallas kernels for 13%

profile of v4, /device:TPU:0, one launch (start us, length us, event | category | flops | bytes accessed | tf_op | source)
XLA Modules:
  0.0 56.8 jit_solution(15079715272397189704)
XLA Ops:
  0.6 28.2 %horner_and_gradient.1 = (f32[16,2,16,2,8,128]{5,4,3,2,1,0:T(8,128)}, bf16[640,128]{1,0:T(8,128)(2,1)}) custom-call(f32[16,7]{1,0:T(8,128)} %constant.12.clone.factor_ref, bf16[8,32,32,128]{3,2,1,0:T(8,128)(2,1)} %x_ref.1, bf16[8,32,32,128]{3,2,1,0:T(8,128)(2,1)} %t_hbm.1, f32[3,3,128,128]{3,2,1,0:T(8,128)} %kernel_hbm.1, ...), custom_call_target="tpu_custom_call" | custom-call | flops 22548578304 | bytes 12582912 | tf_op jit(solution)/shard_map/horner_and_gradient/pallas_call | solution.py:353
  28.8 15.2 %all_to_all.10 = bf16[32,10,2,128]{3,2,1,0:T(2,128)(2,1)S(1)} all-to-all(bf16[32,10,2,128]{3,2,1,0:T(2,128)(2,1)} %bitcast.3), channel_id=1, replica_groups=mesh['sample'=4,'freq'=8] {'sample','freq'}, dimensions={0} | all-to-all | bytes 327680 | tf_op jit(solution)/shard_map/all_to_all | solution.py:335
  44.0 0.2 multiply_reduce_fusion
  44.2 0.8 %broadcast_in_dim.2 = bf16[32,10,2,128]{3,2,1,0:T(2,128)(2,1)} broadcast(bf16[10,2,128]{2,1,0:T(2,128)(2,1)S(1)} %multiply_reduce_fusion), dimensions={1,2,3} | broadcast | bytes 168960 | tf_op jit(solution)/shard_map/broadcast_in_dim | solution.py:338
  45.0 3.0 %all-to-all-start.1 = ((bf16[32,10,2,128]{3,2,1,0:T(2,128)(2,1)}), bf16[32,10,2,128]{3,2,1,0:T(2,128)(2,1)S(1)}, u32[]{:S(2)}, u32[]{:S(2)}) async-start(bf16[32,10,2,128]{3,2,1,0:T(2,128)(2,1)} %broadcast_in_dim.2), calls=%async_computation.1 | async-start | bytes 327680 | tf_op jit(solution)/shard_map/all_to_all | solution.py:337
  47.9 7.2 %inverse_transform.1 = bf16[8,32,32,128]{3,2,1,0:T(8,128)(2,1)} custom-call(bf16[8,32,32,128]{3,2,1,0:T(8,128)(2,1)} %x_ref.1, f32[16,2,16,2,8,128]{5,4,3,2,1,0:T(8,128)} %get-tuple-element.4.dev_ref, bf16[256,256]{1,0:T(8,128)(2,1)} %constant.14.clone.high_ref, bf16[256,256]{1,0:T(8,128)(2,1)} %constant.15.clone.low_ref), custom_call_target="tpu_custom_call" | custom-call | flops 1610612736 | bytes 8388608 | tf_op jit(solution)/shard_map/inverse_transform/pallas_call | solution.py:393
  55.2 0.7 %all-to-all-done.1 = bf16[32,10,2,128]{3,2,1,0:T(2,128)(2,1)S(1)} async-done(((bf16[32,10,2,128]{3,2,1,0:T(2,128)(2,1)}), bf16[32,10,2,128]{3,2,1,0:T(2,128)(2,1)S(1)}, u32[]{:S(2)}, u32[]{:S(2)}) %all-to-all-start.1) | async-done | bytes 163872 | tf_op jit(solution)/shard_map/all_to_all | solution.py:337
  55.9 0.9 %mirror_taps.1 = f32[3,3,128,128]{3,2,1,0:T(8,128)} custom-call(bf16[640,128]{1,0:T(8,128)(2,1)S(1)} %bitcast.2), custom_call_target="tpu_custom_call" | custom-call | tf_op jit(solution)/shard_map/mirror_taps/pallas_call | solution.py:406
Async XLA Ops:
  45.0 10.9 %all-to-all-start.1 = ((bf16[32,10,2,128]{3,2,1,0:T(2,128)(2,1)}), bf16[32,10,2,128]{3,2,1,0:T(2,128)(2,1)S(1)}, u32[]{:S(2)}, u32[]{:S(2)}) async-start(bf16[32,10,2,128]{3,2,1,0:T(2,128)(2,1)} %broadcast_in_dim.2), calls=%async_computation.1 | async-start | bytes 327680 | tf_op jit(solution)/shard_map/all_to_all | solution.py:337

commit v5 on v4

--- a/solution.py
+++ b/solution.py
@@ -14,7 +14,7 @@
 CHAINS = 2
 IN_PARTS = 4
 AHEAD = 2
-UNROLL = 8
+LAG = 0
 GROUPS = 2
 HALF_TAPS = ((1, 1), (1, 2), (2, 0), (2, 1), (2, 2))
 VMEM_LIMIT = 56 * 1024 * 1024
@@ -113,11 +113,8 @@
     for place in range(AHEAD):
         for index in range(2):
             incoming(index, place).start()
-    kernel_copy.start()
-    sums_ref[...] = jnp.zeros_like(sums_ref)
-    left_ref[...] = jnp.zeros_like(left_ref)
-    right_ref[...] = jnp.zeros_like(right_ref)
-
+        if place == 0:
+            kernel_copy.start()
     def make_taps():
         for a in range(3):
             flipped = [kernel_ref[a, b].T - kernel_ref[2 - a, 2 - b] for b in range(3)]
@@ -130,7 +127,7 @@
         taps_ref[1] = outside + inside
         taps_ref[2] = outside - inside
 
-    def transform(h, carry):
+    def transform(h):
         rows = jnp.concatenate(
             [
                 x_ref[:, h].reshape(number * side, channels),
@@ -146,7 +143,6 @@
         base_ref[:, odd, pair, :number, channels:] = result[:, 1, :, :channels]
         base_ref[:, odd, pair, number:, :channels] = result[:, 0, :, channels:]
         base_ref[:, odd, pair, number:, channels:] = result[:, 1, :, channels:]
-        return carry
 
     def before_of(rows):
         return jnp.concatenate([rows[pairs - 1 :], rows[: pairs - 1]], axis=0)
@@ -161,19 +157,21 @@
         held_ref[chain, parity, 2] = odd - even
         held_ref[chain, parity, 3] = even - after_of(even)
 
-    def prepare_taps(buffer, slot, a):
+    def prepare_taps(slot, a):
         cos_top, cos_low, sine = (factor_ref[slot, j] for j in range(3))
         first, second = taps_ref[a, 0], taps_ref[a, 1]
         cross = (sine * taps_ref[a, 2]).astype(jnp.bfloat16)
-        weight_ref[buffer, a, :channels, :channels] = (first + cos_top * second).astype(jnp.bfloat16)
-        weight_ref[buffer, a, channels:, channels:] = (first + cos_low * second).astype(jnp.bfloat16)
-        weight_ref[buffer, a, :channels, channels:] = cross
-        weight_ref[buffer, a, channels:, :channels] = -cross
-
-    def apply(buffer, chain, parity, slot):
+        top = (first + cos_top * second).astype(jnp.bfloat16)
+        low = top if slot else (first + cos_low * second).astype(jnp.bfloat16)
+        weight_ref[slot, a, :channels, :channels] = top
+        weight_ref[slot, a, channels:, channels:] = low
+        weight_ref[slot, a, :channels, channels:] = cross
+        weight_ref[slot, a, channels:, :channels] = -cross
+
+    def apply(chain, parity, slot):
         def part(place):
             left = held_ref[chain, parity, place].reshape(pairs * 2 * number, wide)
-            return dot(left, weight_ref[buffer, place]).reshape(pairs, 2 * number, wide)
+            return dot(left, weight_ref[slot, place]).reshape(pairs, 2 * number, wide)
 
         first, inner, outer, last = (part(place) for place in range(4))
         return first + (inner + outer), (inner - outer) - last
@@ -221,18 +219,10 @@
         there = CHAINS - here
         before = jnp.maximum((group - 1) * CHAINS, 0)
         after = jnp.minimum((group + 1) * CHAINS, slots - CHAINS)
-        jobs = [
-            functools.partial(products, there + chain, before + chain) for chain in range(CHAINS)
-        ] + [
-            functools.partial(prepare_taps, there + chain, after + chain, a)
-            for chain in range(CHAINS)
-            for a in range(4)
-        ]
-        share = -(-len(jobs) // ((APPLICATIONS - 1) * CHAINS))
         for step in range(APPLICATIONS):
             for chain in range(CHAINS):
                 slot = group * CHAINS + chain
-                even, odd = apply(here + chain, chain, (first + step) % 2, slot)
+                even, odd = apply(chain, (first + step) % 2, slot)
                 even_new = advance(even, base_ref[slot, 0], step)
                 odd_new = advance(odd, base_ref[slot, 1], step)
                 if step < APPLICATIONS - 1:
@@ -248,10 +238,13 @@
                     store_held(
                         chain, 1 - first, base_ref[after + chain, 0], base_ref[after + chain, 1]
                     )
-                for job in jobs[:share]:
-                    job()
-                jobs = jobs[share:]
-
+                if step == LAG:
+                    products(there + chain, before + chain)
+
+    sums_ref[...] = jnp.zeros_like(sums_ref)
+    left_ref[CHAINS:] = jnp.zeros_like(left_ref[CHAINS:])
+    right_ref[CHAINS:] = jnp.zeros_like(right_ref[CHAINS:])
+    jobs = [(slot, a) for slot in range(slots) for a in range(4)]
     table_copy.wait()
     for place in range(IN_PARTS):
         for index in range(2):
@@ -262,18 +255,20 @@
         if place == 1:
             kernel_copy.wait()
             make_taps()
-            for chain in range(CHAINS):
-                for a in range(4):
-                    prepare_taps(chain, chain, a)
-        lax.fori_loop(place * part, (place + 1) * part, transform, 0, unroll=UNROLL)
+        for h in range(place * part, (place + 1) * part):
+            transform(h)
+            if place:
+                turn, turns = h - part, side - part
+                for job in jobs[turn * len(jobs) // turns : (turn + 1) * len(jobs) // turns]:
+                    prepare_taps(*job)
     for chain in range(CHAINS):
         store_held(chain, 0, base_ref[chain, 0], base_ref[chain, 1])
 
     def some_groups(index, carry):
         for member in range(GROUPS):
             work(GROUPS * index + member, member % 2 == 1)
-        for slot in range(GROUPS * CHAINS):
-            outgoing(index * GROUPS * CHAINS + slot).start()
+            for chain in range(CHAINS):
+                outgoing((index * GROUPS + member) * CHAINS + chain).start()
         return carry
 
     lax.fori_loop(0, slots // (GROUPS * CHAINS), some_groups, 0)
@@ -365,7 +360,7 @@
             pltpu.VMEM(forward_both.shape, jnp.bfloat16),
             pltpu.VMEM((slots, 2, side // 2, 2 * number, wide), jnp.float32),
             pltpu.VMEM((CHAINS, 2, 4, side // 2, 2 * number, wide), jnp.bfloat16),
-            pltpu.VMEM((2 * CHAINS, 4, wide, wide), jnp.bfloat16),
+            pltpu.VMEM((slots, 4, wide, wide), jnp.bfloat16),
             pltpu.VMEM((4, 3, channels, channels), jnp.float32),
             pltpu.VMEM((3, 3, channels, channels), jnp.float32),
             pltpu.VMEM((slots, 2, side // 2, 2, number, channels), jnp.float32),

time: 57.1 us -> 55.8 us (0.977)
  Pallas kernels: 36.3 us -> 35 us
    pallas_call x1, Pallas kernels: 28.2 us -> 26.8 us  [per_device(): pl.pallas_call(main_kernel, out_shape=(jax.ShapeDtypeStruct((slots, 2, si...]
where the time goes in v5:
time: 55.8 us; the launch traced here: 55.5 us
  Pallas kernels  35 us (63%)
  blocking collectives  15.2 us (27%)
  starting transfers between devices  2.98 us (5%)
  local copies, waits for them, and re-layouts  0.75 us (1%)
  waiting for transfers between devices  0.69 us (1%)
  between operations  0.65 us (1%)
    pallas_call x1, Pallas kernels, per_device(): pl.pallas_call(main_kernel, out_shape=(jax.ShapeDtypeStruct((slots, 2, si...  26.8 us
    all_to_all x1, blocking collectives, device_sum(): lax.all_to_all(pieces, AXES, split_axis=0, concat_axis=0, tiled=True)  15.2 us
    pallas_call x1, Pallas kernels, per_device(): pl.pallas_call(inverse_kernel, out_shape=jax.ShapeDtypeStruct(images.shap...  7.23 us
    all_to_all x1, starting transfers between devices, device_sum(): lax.all_to_all(jnp.broadcast_to(own, terms.shape), AXES, split_axis=0, co...  2.98 us
  transfers between devices with their start and end apart: 1, of which 1 were waited for; matrix products, arithmetic and copies ran while one was open for 0% of the time, Pallas kernels for 13%

profile of v5, /device:TPU:0, one launch (start us, length us, event | category | flops | bytes accessed | tf_op | source)
XLA Modules:
  0.0 55.5 jit_solution(2309512876523203483)
XLA Ops:
  0.6 26.8 %horner_and_gradient.1 = (f32[16,2,16,2,8,128]{5,4,3,2,1,0:T(8,128)}, bf16[640,128]{1,0:T(8,128)(2,1)}) custom-call(f32[16,7]{1,0:T(8,128)} %constant.12.clone.factor_ref, bf16[8,32,32,128]{3,2,1,0:T(8,128)(2,1)} %x_ref.1, bf16[8,32,32,128]{3,2,1,0:T(8,128)(2,1)} %t_hbm.1, f32[3,3,128,128]{3,2,1,0:T(8,128)} %kernel_hbm.1, ...), custom_call_target="tpu_custom_call" | custom-call | flops 22548578304 | bytes 12582912 | tf_op jit(solution)/shard_map/horner_and_gradient/pallas_call | solution.py:348
  27.5 15.2 %all_to_all.10 = bf16[32,10,2,128]{3,2,1,0:T(2,128)(2,1)S(1)} all-to-all(bf16[32,10,2,128]{3,2,1,0:T(2,128)(2,1)} %bitcast.3), channel_id=1, replica_groups=mesh['sample'=4,'freq'=8] {'sample','freq'}, dimensions={0} | all-to-all | bytes 327680 | tf_op jit(solution)/shard_map/all_to_all | solution.py:330
  42.7 0.2 multiply_reduce_fusion
  42.9 0.8 %broadcast_in_dim.2 = bf16[32,10,2,128]{3,2,1,0:T(2,128)(2,1)} broadcast(bf16[10,2,128]{2,1,0:T(2,128)(2,1)S(1)} %multiply_reduce_fusion), dimensions={1,2,3} | broadcast | bytes 168960 | tf_op jit(solution)/shard_map/broadcast_in_dim | solution.py:333
  43.6 3.0 %all-to-all-start.1 = ((bf16[32,10,2,128]{3,2,1,0:T(2,128)(2,1)}), bf16[32,10,2,128]{3,2,1,0:T(2,128)(2,1)S(1)}, u32[]{:S(2)}, u32[]{:S(2)}) async-start(bf16[32,10,2,128]{3,2,1,0:T(2,128)(2,1)} %broadcast_in_dim.2), calls=%async_computation.1 | async-start | bytes 327680 | tf_op jit(solution)/shard_map/all_to_all | solution.py:332
  46.6 7.2 %inverse_transform.1 = bf16[8,32,32,128]{3,2,1,0:T(8,128)(2,1)} custom-call(bf16[8,32,32,128]{3,2,1,0:T(8,128)(2,1)} %x_ref.1, f32[16,2,16,2,8,128]{5,4,3,2,1,0:T(8,128)} %get-tuple-element.4.dev_ref, bf16[256,256]{1,0:T(8,128)(2,1)} %constant.14.clone.high_ref, bf16[256,256]{1,0:T(8,128)(2,1)} %constant.15.clone.low_ref), custom_call_target="tpu_custom_call" | custom-call | flops 1610612736 | bytes 8388608 | tf_op jit(solution)/shard_map/inverse_transform/pallas_call | solution.py:388
  53.9 0.7 %all-to-all-done.1 = bf16[32,10,2,128]{3,2,1,0:T(2,128)(2,1)S(1)} async-done(((bf16[32,10,2,128]{3,2,1,0:T(2,128)(2,1)}), bf16[32,10,2,128]{3,2,1,0:T(2,128)(2,1)S(1)}, u32[]{:S(2)}, u32[]{:S(2)}) %all-to-all-start.1) | async-done | bytes 163872 | tf_op jit(solution)/shard_map/all_to_all | solution.py:332
  54.6 0.9 %mirror_taps.1 = f32[3,3,128,128]{3,2,1,0:T(8,128)} custom-call(bf16[640,128]{1,0:T(8,128)(2,1)S(1)} %bitcast.2), custom_call_target="tpu_custom_call" | custom-call | tf_op jit(solution)/shard_map/mirror_taps/pallas_call | solution.py:401
Async XLA Ops:
  43.6 10.9 %all-to-all-start.1 = ((bf16[32,10,2,128]{3,2,1,0:T(2,128)(2,1)}), bf16[32,10,2,128]{3,2,1,0:T(2,128)(2,1)S(1)}, u32[]{:S(2)}, u32[]{:S(2)}) async-start(bf16[32,10,2,128]{3,2,1,0:T(2,128)(2,1)} %broadcast_in_dim.2), calls=%async_computation.1 | async-start | bytes 327680 | tf_op jit(solution)/shard_map/all_to_all | solution.py:332

commit v6 on v5

--- a/solution.py
+++ b/solution.py
@@ -15,8 +15,8 @@
 IN_PARTS = 4
 AHEAD = 2
 LAG = 0
-GROUPS = 2
-HALF_TAPS = ((1, 1), (1, 2), (2, 0), (2, 1), (2, 2))
+GROUPS = 4
+HALF_TAPS = ((1, 2), (2, 0), (2, 1), (2, 2))
 VMEM_LIMIT = 56 * 1024 * 1024
 MIRROR_LIMIT = 4 * 1024 * 1024
 
@@ -135,9 +135,7 @@
             ],
             axis=1,
         )
-        both = dot(table_ref[...], rows)
-        half = side * number
-        result = (both[:half] + both[half:]).reshape(slots, 2, number, wide)
+        result = dot(table_ref[...], rows).reshape(slots, 2, number, wide)
         pair, odd = h // 2, h % 2
         base_ref[:, odd, pair, :number, :channels] = result[:, 0, :, :channels]
         base_ref[:, odd, pair, :number, channels:] = result[:, 1, :, :channels]
@@ -282,10 +280,18 @@
             return sums_ref[a, 1] - sums_ref[a, 2]
         return sums_ref[a, 1] + sums_ref[a, 2]
 
+    half = channels // 2
+    centre = correlation(1, 1)
+    centre = centre - centre.T
+    row = lax.broadcasted_iota(jnp.int32, (half, channels), 0)
+    lane = lax.broadcasted_iota(jnp.int32, (half, channels), 1)
+    packed = jnp.where(lane > row, centre[:half], pltpu.roll(centre[half:], half, 1))
+    grad_ref[:half] = packed.astype(grad_ref.dtype)
     for place, (a, b) in enumerate(HALF_TAPS):
         piece = correlation(a, b) - correlation(2 - a, 2 - b).T
-        grad_ref[place * channels : (place + 1) * channels] = piece.astype(grad_ref.dtype)
-    rows = len(HALF_TAPS) * channels
+        start = half + place * channels
+        grad_ref[start : start + channels] = piece.astype(grad_ref.dtype)
+    rows = half + len(HALF_TAPS) * channels
     if grad_ref.shape[0] > rows:
         grad_ref[rows:] = jnp.zeros((grad_ref.shape[0] - rows, channels), grad_ref.dtype)
     for slot in range(slots):
@@ -314,11 +320,19 @@
 
 def mirror_kernel(sum_ref, grad_ref):
     channels = sum_ref.shape[1]
+    half = channels // 2
+    packed = sum_ref[:half].astype(jnp.float32)
+    row = lax.broadcasted_iota(jnp.int32, (half, channels), 0)
+    lane = lax.broadcasted_iota(jnp.int32, (half, channels), 1)
+    upper = jnp.where(lane > row, packed, 0.0)
+    lower = pltpu.roll(jnp.where(lane < row, packed, 0.0), half, 1)
+    once = jnp.concatenate([upper, lower], axis=0)
+    grad_ref[1, 1] = once - once.T
     for place, (a, b) in enumerate(HALF_TAPS):
-        piece = sum_ref[place * channels : (place + 1) * channels].astype(jnp.float32)
+        start = half + place * channels
+        piece = sum_ref[start : start + channels].astype(jnp.float32)
         grad_ref[a, b] = piece
-        if place:
-            grad_ref[2 - a, 2 - b] = -piece.T
+        grad_ref[2 - a, 2 - b] = -piece.T
 
 
 def whole(memory_space=pltpu.VMEM):
@@ -340,8 +354,9 @@
     slots = side // 2
     wide = 2 * channels
     count = lax.axis_size("sample") * lax.axis_size("freq")
-    share = -(-len(HALF_TAPS) * channels // (2 * count)) * 2
-    forward_both = np.concatenate(split_table(forward_table(number, side)), axis=0)
+    sent = channels // 2 + len(HALF_TAPS) * channels
+    share = -(-sent // (2 * count)) * 2
+    forward = forward_table(number, side).astype(jnp.bfloat16)
     inverse_high, inverse_low = split_table(inverse_table(number, side))
     rows = side * 2 * number
     params = pltpu.CompilerParams(vmem_limit_bytes=VMEM_LIMIT)
@@ -357,7 +372,7 @@
             pltpu.VMEM(images.shape, jnp.bfloat16),
             pltpu.VMEM(images.shape, jnp.bfloat16),
             pltpu.VMEM(kernel.shape, jnp.float32),
-            pltpu.VMEM(forward_both.shape, jnp.bfloat16),
+            pltpu.VMEM(forward.shape, jnp.bfloat16),
             pltpu.VMEM((slots, 2, side // 2, 2 * number, wide), jnp.float32),
             pltpu.VMEM((CHAINS, 2, 4, side // 2, 2 * number, wide), jnp.bfloat16),
             pltpu.VMEM((slots, 4, wide, wide), jnp.bfloat16),
@@ -382,7 +397,7 @@
         images,
         cotangent,
         kernel,
-        jnp.asarray(forward_both),
+        jnp.asarray(forward),
     )
     summed = device_sum(partial, 2.0 / (number * count), count)
     outputs = pl.pallas_call(

time: 55.8 us -> 54.4 us (0.975)
  Pallas kernels: 35 us -> 34 us
    pallas_call x1, Pallas kernels: 26.8 us -> 25.8 us  [per_device(): pl.pallas_call(main_kernel, out_shape=(jax.ShapeDtypeStruct((slots, 2, si...]
where the time goes in v6:
time: 54.4 us; the launch traced here: 54.1 us
  Pallas kernels  34 us (62%)
  blocking collectives  15.1 us (28%)
  starting transfers between devices  2.72 us (5%)
  local copies, waits for them, and re-layouts  0.74 us (1%)
  between operations  0.65 us (1%)
  waiting for transfers between devices  0.6 us (1%)
    pallas_call x1, Pallas kernels, per_device(): pl.pallas_call(main_kernel, out_shape=(jax.ShapeDtypeStruct((slots, 2, si...  25.8 us
    all_to_all x1, blocking collectives, device_sum(): lax.all_to_all(pieces, AXES, split_axis=0, concat_axis=0, tiled=True)  15.1 us
    pallas_call x1, Pallas kernels, per_device(): pl.pallas_call(inverse_kernel, out_shape=jax.ShapeDtypeStruct(images.shap...  7.22 us
    all_to_all x1, starting transfers between devices, device_sum(): lax.all_to_all(jnp.broadcast_to(own, terms.shape), AXES, split_axis=0, co...  2.72 us
  transfers between devices with their start and end apart: 1, of which 1 were waited for; matrix products, arithmetic and copies ran while one was open for 0% of the time, Pallas kernels for 13%

profile of v6, /device:TPU:0, one launch (start us, length us, event | category | flops | bytes accessed | tf_op | source)
XLA Modules:
  0.0 54.1 jit_solution(13702506810770193415)
XLA Ops:
  0.6 25.8 %horner_and_gradient.1 = (f32[16,2,16,2,8,128]{5,4,3,2,1,0:T(8,128)}, bf16[576,128]{1,0:T(8,128)(2,1)}) custom-call(f32[16,7]{1,0:T(8,128)} %constant.12.clone.factor_ref, bf16[8,32,32,128]{3,2,1,0:T(8,128)(2,1)} %x_ref.1, bf16[8,32,32,128]{3,2,1,0:T(8,128)(2,1)} %t_hbm.1, f32[3,3,128,128]{3,2,1,0:T(8,128)} %kernel_hbm.1, ...), custom_call_target="tpu_custom_call" | custom-call | flops 22548578304 | bytes 12582912 | tf_op jit(solution)/shard_map/horner_and_gradient/pallas_call | solution.py:363
  26.5 15.1 %all_to_all.10 = bf16[32,9,2,128]{3,2,1,0:T(2,128)(2,1)S(1)} all-to-all(bf16[32,9,2,128]{3,2,1,0:T(2,128)(2,1)} %bitcast.3), channel_id=1, replica_groups=mesh['sample'=4,'freq'=8] {'sample','freq'}, dimensions={0} | all-to-all | bytes 294912 | tf_op jit(solution)/shard_map/all_to_all | solution.py:344
  41.6 0.2 multiply_reduce_fusion
  41.8 0.7 %broadcast_in_dim.2 = bf16[32,9,2,128]{3,2,1,0:T(2,128)(2,1)} broadcast(bf16[9,2,128]{2,1,0:T(2,128)(2,1)S(1)} %multiply_reduce_fusion), dimensions={1,2,3} | broadcast | bytes 152064 | tf_op jit(solution)/shard_map/broadcast_in_dim | solution.py:347
  42.5 2.7 %all-to-all-start.1 = ((bf16[32,9,2,128]{3,2,1,0:T(2,128)(2,1)}), bf16[32,9,2,128]{3,2,1,0:T(2,128)(2,1)S(1)}, u32[]{:S(2)}, u32[]{:S(2)}) async-start(bf16[32,9,2,128]{3,2,1,0:T(2,128)(2,1)} %broadcast_in_dim.2), calls=%async_computation.1 | async-start | bytes 294912 | tf_op jit(solution)/shard_map/all_to_all | solution.py:346
  45.2 7.2 %inverse_transform.1 = bf16[8,32,32,128]{3,2,1,0:T(8,128)(2,1)} custom-call(bf16[8,32,32,128]{3,2,1,0:T(8,128)(2,1)} %x_ref.1, f32[16,2,16,2,8,128]{5,4,3,2,1,0:T(8,128)} %get-tuple-element.4.dev_ref, bf16[256,256]{1,0:T(8,128)(2,1)} %constant.14.clone.high_ref, bf16[256,256]{1,0:T(8,128)(2,1)} %constant.15.clone.low_ref), custom_call_target="tpu_custom_call" | custom-call | flops 1610612736 | bytes 8388608 | tf_op jit(solution)/shard_map/inverse_transform/pallas_call | solution.py:403
  52.5 0.6 %all-to-all-done.1 = bf16[32,9,2,128]{3,2,1,0:T(2,128)(2,1)S(1)} async-done(((bf16[32,9,2,128]{3,2,1,0:T(2,128)(2,1)}), bf16[32,9,2,128]{3,2,1,0:T(2,128)(2,1)S(1)}, u32[]{:S(2)}, u32[]{:S(2)}) %all-to-all-start.1) | async-done | bytes 147488 | tf_op jit(solution)/shard_map/all_to_all | solution.py:346
  53.1 1.0 %mirror_taps.1 = f32[3,3,128,128]{3,2,1,0:T(8,128)} custom-call(bf16[576,128]{1,0:T(8,128)(2,1)S(1)} %bitcast.2), custom_call_target="tpu_custom_call" | custom-call | tf_op jit(solution)/shard_map/mirror_taps/pallas_call | solution.py:416
Async XLA Ops:
  42.5 10.6 %all-to-all-start.1 = ((bf16[32,9,2,128]{3,2,1,0:T(2,128)(2,1)}), bf16[32,9,2,128]{3,2,1,0:T(2,128)(2,1)S(1)}, u32[]{:S(2)}, u32[]{:S(2)}) async-start(bf16[32,9,2,128]{3,2,1,0:T(2,128)(2,1)} %broadcast_in_dim.2), calls=%async_computation.1 | async-start | bytes 294912 | tf_op jit(solution)/shard_map/all_to_all | solution.py:346

commit v7 on v6

--- a/solution.py
+++ b/solution.py
@@ -239,9 +239,6 @@
                 if step == LAG:
                     products(there + chain, before + chain)
 
-    sums_ref[...] = jnp.zeros_like(sums_ref)
-    left_ref[CHAINS:] = jnp.zeros_like(left_ref[CHAINS:])
-    right_ref[CHAINS:] = jnp.zeros_like(right_ref[CHAINS:])
     jobs = [(slot, a) for slot in range(slots) for a in range(4)]
     table_copy.wait()
     for place in range(IN_PARTS):
@@ -253,6 +250,9 @@
         if place == 1:
             kernel_copy.wait()
             make_taps()
+            sums_ref[...] = jnp.zeros_like(sums_ref)
+            left_ref[CHAINS:] = jnp.zeros_like(left_ref[CHAINS:])
+            right_ref[CHAINS:] = jnp.zeros_like(right_ref[CHAINS:])
         for h in range(place * part, (place + 1) * part):
             transform(h)
             if place:

time: 54.4 us -> 54.4 us (level)
  no operation moved by 1% of the time
where the time goes in v7:
time: 54.4 us; the launch traced here: 54.1 us
  Pallas kernels  34.1 us (63%)
  blocking collectives  15.1 us (28%)
  starting transfers between devices  2.72 us (5%)
  local copies, waits for them, and re-layouts  0.74 us (1%)
  between operations  0.65 us (1%)
  waiting for transfers between devices  0.6 us (1%)
    pallas_call x1, Pallas kernels, per_device(): pl.pallas_call(main_kernel, out_shape=(jax.ShapeDtypeStruct((slots, 2, si...  25.9 us
    all_to_all x1, blocking collectives, device_sum(): lax.all_to_all(pieces, AXES, split_axis=0, concat_axis=0, tiled=True)  15.1 us
    pallas_call x1, Pallas kernels, per_device(): pl.pallas_call(inverse_kernel, out_shape=jax.ShapeDtypeStruct(images.shap...  7.23 us
    all_to_all x1, starting transfers between devices, device_sum(): lax.all_to_all(jnp.broadcast_to(own, terms.shape), AXES, split_axis=0, co...  2.72 us
  transfers between devices with their start and end apart: 1, of which 1 were waited for; matrix products, arithmetic and copies ran while one was open for 0% of the time, Pallas kernels for 13%

profile of v7, /device:TPU:0, one launch (start us, length us, event | category | flops | bytes accessed | tf_op | source)
XLA Modules:
  0.0 54.1 jit_solution(15532009343141131136)
XLA Ops:
  0.6 25.9 %horner_and_gradient.1 = (f32[16,2,16,2,8,128]{5,4,3,2,1,0:T(8,128)}, bf16[576,128]{1,0:T(8,128)(2,1)}) custom-call(f32[16,7]{1,0:T(8,128)} %constant.12.clone.factor_ref, bf16[8,32,32,128]{3,2,1,0:T(8,128)(2,1)} %x_ref.1, bf16[8,32,32,128]{3,2,1,0:T(8,128)(2,1)} %t_hbm.1, f32[3,3,128,128]{3,2,1,0:T(8,128)} %kernel_hbm.1, ...), custom_call_target="tpu_custom_call" | custom-call | flops 22548578304 | bytes 12582912 | tf_op jit(solution)/shard_map/horner_and_gradient/pallas_call | solution.py:363
  26.5 15.1 %all_to_all.10 = bf16[32,9,2,128]{3,2,1,0:T(2,128)(2,1)S(1)} all-to-all(bf16[32,9,2,128]{3,2,1,0:T(2,128)(2,1)} %bitcast.3), channel_id=1, replica_groups=mesh['sample'=4,'freq'=8] {'sample','freq'}, dimensions={0} | all-to-all | bytes 294912 | tf_op jit(solution)/shard_map/all_to_all | solution.py:344
  41.6 0.2 multiply_reduce_fusion
  41.8 0.7 %broadcast_in_dim.2 = bf16[32,9,2,128]{3,2,1,0:T(2,128)(2,1)} broadcast(bf16[9,2,128]{2,1,0:T(2,128)(2,1)S(1)} %multiply_reduce_fusion), dimensions={1,2,3} | broadcast | bytes 152064 | tf_op jit(solution)/shard_map/broadcast_in_dim | solution.py:347
  42.6 2.7 %all-to-all-start.1 = ((bf16[32,9,2,128]{3,2,1,0:T(2,128)(2,1)}), bf16[32,9,2,128]{3,2,1,0:T(2,128)(2,1)S(1)}, u32[]{:S(2)}, u32[]{:S(2)}) async-start(bf16[32,9,2,128]{3,2,1,0:T(2,128)(2,1)} %broadcast_in_dim.2), calls=%async_computation.1 | async-start | bytes 294912 | tf_op jit(solution)/shard_map/all_to_all | solution.py:346
  45.3 7.2 %inverse_transform.1 = bf16[8,32,32,128]{3,2,1,0:T(8,128)(2,1)} custom-call(bf16[8,32,32,128]{3,2,1,0:T(8,128)(2,1)} %x_ref.1, f32[16,2,16,2,8,128]{5,4,3,2,1,0:T(8,128)} %get-tuple-element.4.dev_ref, bf16[256,256]{1,0:T(8,128)(2,1)} %constant.14.clone.high_ref, bf16[256,256]{1,0:T(8,128)(2,1)} %constant.15.clone.low_ref), custom_call_target="tpu_custom_call" | custom-call | flops 1610612736 | bytes 8388608 | tf_op jit(solution)/shard_map/inverse_transform/pallas_call | solution.py:403
  52.5 0.6 %all-to-all-done.1 = bf16[32,9,2,128]{3,2,1,0:T(2,128)(2,1)S(1)} async-done(((bf16[32,9,2,128]{3,2,1,0:T(2,128)(2,1)}), bf16[32,9,2,128]{3,2,1,0:T(2,128)(2,1)S(1)}, u32[]{:S(2)}, u32[]{:S(2)}) %all-to-all-start.1) | async-done | bytes 147488 | tf_op jit(solution)/shard_map/all_to_all | solution.py:346
  53.1 1.0 %mirror_taps.1 = f32[3,3,128,128]{3,2,1,0:T(8,128)} custom-call(bf16[576,128]{1,0:T(8,128)(2,1)S(1)} %bitcast.2), custom_call_target="tpu_custom_call" | custom-call | tf_op jit(solution)/shard_map/mirror_taps/pallas_call | solution.py:416
Async XLA Ops:
  42.6 10.6 %all-to-all-start.1 = ((bf16[32,9,2,128]{3,2,1,0:T(2,128)(2,1)}), bf16[32,9,2,128]{3,2,1,0:T(2,128)(2,1)S(1)}, u32[]{:S(2)}, u32[]{:S(2)}) async-start(bf16[32,9,2,128]{3,2,1,0:T(2,128)(2,1)} %broadcast_in_dim.2), calls=%async_computation.1 | async-start | bytes 294912 | tf_op jit(solution)/shard_map/all_to_all | solution.py:346
